TPU v7x, 32 devices: a whole 2x2x4 slice. The times are simulated.
32 devices in a mesh: sens: 16 (over z, x, core), hour: 2 (over y).
Axes of the slice: x: 2, y: 2, z: 4, core: 2. Of those that a mesh axis runs over, the one named last changes fastest.
Arguments:
- windows: bfloat16 [2, 128, 3, 4096], P('hour', 'sens'), may hold values from -6 to 6
- pair_first: int32 [1024], P('sens'), may hold values from 0 to 7
- pair_second: int32 [1024], P('sens'), may hold values from 0 to 23
- owners: int32 [1024, 1], P('sens'), may hold values from 0 to 15; in each aligned block of 64 rows (0 to 63, 64 to 127, ...) at most 8 rows name the same one
Outputs:
- stacks: float32 [2048, 9216], P('sens', 'hour')
Inputs may be any that keep to these rules, and one draw needn't show every extreme that they name: `owners`: within the 64 pairs of one block no owner appears more than 8 times, and some owner appears exactly 8 times.
All inputs are finite; a program needn't handle non-finite values.
Results may differ from a plain program's by a relative error of at most 0.004.
Values may be sent and summed in bfloat16 or wider, within the bound.
A program may use at most 128 MiB of HBM per device.

v0:
```python
import jax
import jax.numpy as jnp
from jax import lax
from jax.sharding import PartitionSpec as P

SAMPLES = 4096
PADDED = 8192
NB = 2048
LAGS = 1024
COMPS = 3


def from_behind(value, axis, steps):
    count = lax.axis_size(axis)
    pairs = [(source, (source + steps) % count) for source in range(count)]
    return lax.ppermute(value, axis, pairs)


def build_tables():
    times = jnp.arange(SAMPLES, dtype=jnp.int32)
    bins = jnp.arange(NB, dtype=jnp.int32) + 1
    phase = times[:, None] * bins[None, :] % PADDED
    angle = phase.astype(jnp.float32) * (2.0 * jnp.pi / PADDED)
    fwd = jnp.concatenate([jnp.cos(angle), -jnp.sin(angle)], axis=1).astype(jnp.bfloat16)
    shifts = jnp.arange(LAGS, dtype=jnp.int32) - LAGS // 2
    phase_back = bins[:, None] * shifts[None, :] % PADDED
    angle_back = phase_back.astype(jnp.float32) * (2.0 * jnp.pi / PADDED)
    inv = jnp.concatenate([jnp.cos(angle_back), -jnp.sin(angle_back)], axis=0).astype(jnp.bfloat16)
    return (fwd, inv)


def whiten(rows, fwd):
    spec = jnp.dot(rows, fwd, preferred_element_type=jnp.float32)
    real_part = spec[:, :NB]
    imag_part = spec[:, NB:]
    power = real_part * real_part + imag_part * imag_part
    level = jnp.mean(power, axis=1, keepdims=True)
    scale = 1.0 / jnp.sqrt(power + 0.1 * level + 1e-06)
    return jnp.concatenate([real_part * scale, imag_part * scale], axis=1).astype(jnp.bfloat16)


def shards(windows, pair_first, pair_second, owners):
    hours_here = windows.shape[0]
    sensors_here = windows.shape[1]
    pairs_here = pair_first.shape[0]
    width = COMPS * COMPS * LAGS
    fwd, inv = build_tables()
    white = whiten(windows.reshape(hours_here * sensors_here * COMPS, SAMPLES), fwd)
    white = white.reshape(hours_here, sensors_here, COMPS, 2 * NB)
    nearer = from_behind(white, "sens", -1)
    farther = from_behind(nearer, "sens", -1)
    candidates = jnp.concatenate([white, nearer, farther], axis=1)
    first_spec = jnp.take(white, pair_first, axis=1)
    second_spec = jnp.take(candidates, pair_second, axis=1)
    ar = first_spec[..., :NB].astype(jnp.float32)
    ai = first_spec[..., NB:].astype(jnp.float32)
    br = second_spec[..., :NB].astype(jnp.float32)
    bi = second_spec[..., NB:].astype(jnp.float32)
    real_part = (
        ar[:, :, :, None, :] * br[:, :, None, :, :] + ai[:, :, :, None, :] * bi[:, :, None, :, :]
    )
    imag_part = (
        ar[:, :, :, None, :] * bi[:, :, None, :, :] - ai[:, :, :, None, :] * br[:, :, None, :, :]
    )
    cross = jnp.concatenate([real_part, imag_part], axis=-1).astype(jnp.bfloat16)
    lagged = jnp.dot(
        cross.reshape(hours_here * pairs_here * COMPS * COMPS, 2 * NB),
        inv,
        preferred_element_type=jnp.float32,
    )
    summed = jnp.sum(lagged.reshape(hours_here, pairs_here, width), axis=0)
    owner_count = lax.axis_size("sens")
    capacity = max(2, 2 * pairs_here // owner_count)
    owner = owners[:, 0]
    same = owner[:, None] == owner[None, :]
    order = jnp.arange(pairs_here, dtype=jnp.int32)
    earlier = order[None, :] < order[:, None]
    slot = jnp.sum((same & earlier).astype(jnp.int32), axis=1)
    target = owner * capacity + slot
    outgoing = jnp.zeros((owner_count * capacity, width), jnp.float32).at[target].set(summed)
    received = lax.all_to_all(outgoing, "sens", split_axis=0, concat_axis=0, tiled=True)
    stacked = lax.psum_scatter(received, "hour", scatter_dimension=1, tiled=True)
    all_hours = hours_here * lax.axis_size("hour")
    return stacked / jnp.sqrt(jnp.float32(NB * all_hours))


def solution(mesh):
    placed = (P("hour", "sens", None, None), P("sens"), P("sens"), P("sens", None))
    return jax.shard_map(
        shards, mesh=mesh, in_specs=placed, out_specs=P("sens", "hour"), check_vma=False
    )
```

profile of v0, /device:TPU:0, one launch (start us, length us, event | category | flops | bytes accessed | tf_op | source)
XLA Modules:
  0.0 428.0 jit_solution(1734268262957455615)
XLA Ops:
  6.5 0.0 reduce-scatter.2.cloned.1.call-start
  6.5 0.0 copy-start
  6.5 136.1 %cosine_convert_fusion = (bf16[4096,2048]{1,0:T(8,128)(2,1)}, bf16[4096,2048]{1,0:T(8,128)(2,1)}) fusion(s32[2048]{0:T(1024)S(1)} %iota_add_fusion), kind=kLoop, calls=%fused_computation.14 | loop fusion | flops 142606336 | bytes 33562624 | tf_op jit(solution)/shard_map/convert.14
  142.7 0.0 copy-done
  142.7 0.2 copy.6
  142.8 0.2 reshape.132
  143.0 0.0 copy-start.1
  143.0 0.0 copy-start.3
  143.0 12.1 %fusion.20 = f32[24,4096]{1,0:T(8,128)S(1)} fusion(bf16[24,4096]{1,0:T(8,128)(2,1)S(1)} %reshape.132, bf16[4096,2048]{1,0:T(8,128)(2,1)} %get-tuple-element.16, bf16[4096,2048]{1,0:T(8,128)(2,1)} %get-tuple-element.15), kind=kOutput, calls=%fused_computation.37 | convolution fusion | flops 872415232 | bytes 34144256 | tf_op jit(solution)/shard_map/dot_general | solution.py:33
  155.1 0.0 copy-start.2
  155.1 0.1 fusion.33
  155.3 0.1 multiply_convert_fusion
  155.4 0.1 concatenate.34
  155.5 0.1 concatenate.35
  155.6 0.1 constant_dynamic-update-slice_fusion
  155.7 5.6 %collective-permute-start = (bf16[1,8,3,4096]{3,2,1,0:T(4,128)(2,1)S(1)}, bf16[1,8,3,4096]{3,2,1,0:T(4,128)(2,1)S(1)}, u32[]{:S(2)}, u32[]{:S(2)}) collective-permute-start(bf16[1,8,3,4096]{3,2,1,0:T(4,128)(2,1)S(1)} %constant_dynamic-update-slice_fusion), channel_id=1, source_target_pairs={{0,30},{2,0},{4,2},{6,4},{8,6},{10,8},{12,10},{14,12},{16,14},{18,... | collective-permute-start | bytes 589832 | tf_op jit(solution)/shard_map/ppermute | solution.py:16
  161.3 0.0 copy-done.1
  161.3 0.0 copy-done.3
  161.4 35.9 %cosine_convert_fusion.1 = (bf16[2048,1024]{1,0:T(8,128)(2,1)}, bf16[2048,1024]{1,0:T(8,128)(2,1)}) fusion(s32[1024]{0:T(1024)S(1)} %iota_add_fusion.1, s32[2048]{0:T(1024)S(1)} %iota_add_fusion), kind=kLoop, calls=%fused_computation.31 | loop fusion | flops 35651584 | bytes 8400896 | tf_op jit(solution)/shard_map/convert.4
  197.3 0.0 copy-done.2
  197.3 0.2 convert_reduce_fusion
  197.5 2.4 gather_fusion
  199.8 2.4 bitcast_select_fusion.1
  202.2 0.0 collective-permute-done
  202.2 0.7 collective-permute-start.1
  202.9 3.9 collective-permute-done.1
  206.8 0.5 maximum_bitcast_fusion
  207.3 2.4 gather_fusion.1
  209.7 1.1 bitcast_select_fusion
  210.8 3.2 fusion.27
  214.0 5.2 %add_convert_fusion = (bf16[64,3,3,2048]{3,2,1,0:T(4,128)(2,1)}, bf16[64,3,3,2048]{3,2,1,0:T(4,128)(2,1)S(1)}) fusion(f32[64,3,2048]{2,1,0:T(4,128)S(1)} %get-tuple-element.10, f32[64,3,2048]{2,1,0:T(4,128)S(1)} %get-tuple-element.17, f32[64,3,2048]{2,1,0:T(4,128)S(1)} %get-tuple-element.9, f32[64,3,2048]{2,1,0:T(4,128)S(1)} %get-tuple-element.18), kind=kLoop, calls=%fused_computation.33 | loop fusion | flops 9437184 | bytes 11010048 | tf_op jit(solution)/shard_map/convert.9
  219.2 6.7 %add.110 = bf16[576,2048]{1,0:T(8,128)(2,1)} reshape(bf16[64,3,3,2048]{3,2,1,0:T(4,128)(2,1)} %get-tuple-element.5) | data formatting | bytes 4718592 | tf_op jit(solution)/shard_map/add | solution.py:60
  225.9 4.1 sub.17
  230.0 9.8 %fusion.13 = f32[576,1024]{1,0:T(8,128)S(1)} fusion(bf16[2048,1024]{1,0:T(8,128)(2,1)} %get-tuple-element.14, bf16[2048,1024]{1,0:T(8,128)(2,1)} %get-tuple-element.13, bf16[576,2048]{1,0:T(8,128)(2,1)} %sub.17, bf16[576,2048]{1,0:T(8,128)(2,1)} %add.110), kind=kOutput, calls=%fused_computation.26 | convolution fusion | flops 4858052608 | bytes 15466496 | tf_op jit(solution)/shard_map/dot_general | solution.py:66
  239.9 2.1 reshape.161
  242.0 5.4 %scatter_custom_fusion = f32[128,9216]{1,0:T(8,128)} fusion(s32[64]{0:T(128)S(1)} %fusion.30, f32[64,9216]{1,0:T(8,128)} %reshape.161, f32[]{:T(128)} %constant.41.clone.1), kind=kCustom, calls=%fused_computation.38 | custom fusion | bytes 4719104 | tf_op jit(solution)/shard_map/scatter | solution.py:80
  247.4 109.6 %all_to_all.12 = f32[16,8,9216]{2,1,0:T(8,128)} all-to-all(f32[16,8,9216]{2,1,0:T(8,128)} %bitcast.41), channel_id=1, replica_groups=mesh['sens'=16,'hour'=2] {'sens'}, dimensions={0} | all-to-all | bytes 9437184 | tf_op jit(solution)/shard_map/all_to_all | solution.py:81
  357.0 0.0 reduce-scatter.2.cloned.1.call-update
  357.0 60.8 %reduce-scatter.2.cloned.1.call-done = f32[128,4608]{1,0:T(8,128)} async-done(((f32[128,9216]{1,0:T(8,128)}), f32[128,4608]{1,0:T(8,128)}) %reduce-scatter.2.cloned.1.call-update) | async-done | bytes 2359312 | tf_op jit(solution)/shard_map/reduce_scatter | solution.py:82
  417.8 3.3 broadcast_multiply_fusion
  (11 shorter events, 0.1 us)
Async XLA Ops:
  6.5 411.3 %reduce-scatter.2.cloned.1.call-start = ((), (), s32[]{:S(2)}) async-start(), calls=%async_computation.2 | async-start | bytes 7077888 | tf_op jit(solution)/shard_map/reduce_scatter | solution.py:82
  6.5 136.1 %copy-start = (bf16[1,8,3,4096]{3,1,2,0:T(8,128)(2,1)S(1)}, bf16[1,8,3,4096]{3,1,2,0:T(8,128)(2,1)}, u32[]{:S(2)}) copy-start(bf16[1,8,3,4096]{3,1,2,0:T(8,128)(2,1)} %param.4) | copy-start | bytes 589828
  143.0 18.3 %copy-start.1 = (s32[64]{0:T(128)S(1)}, s32[64]{0:T(128)}, u32[]{:S(2)}) copy-start(s32[64]{0:T(128)} %param.5) | copy-start | bytes 772
  143.0 18.3 %copy-start.3 = (s32[64]{0:T(128)S(1)}, s32[64]{0:T(128)}, u32[]{:S(2)}) copy-start(s32[64]{0:T(128)} %param.6) | copy-start | bytes 772
  155.1 42.2 %copy-start.2 = (s32[64,1]{0,1:T(1,128)S(1)}, s32[64,1]{0,1:T(1,128)}, u32[]{:S(2)}) copy-start(s32[64,1]{0,1:T(1,128)} %param.7) | copy-start | bytes 772
  155.7 46.6 %collective-permute-start = (bf16[1,8,3,4096]{3,2,1,0:T(4,128)(2,1)S(1)}, bf16[1,8,3,4096]{3,2,1,0:T(4,128)(2,1)S(1)}, u32[]{:S(2)}, u32[]{:S(2)}) collective-permute-start(bf16[1,8,3,4096]{3,2,1,0:T(4,128)(2,1)S(1)} %constant_dynamic-update-slice_fusion), channel_id=1, source_target_pairs={{0,30},{2,0},{4,2},{6,4},{8,6},{10,8},{12,10},{14,12},{16,14},{18,... | collective-permute-start | bytes 589832 | tf_op jit(solution)/shard_map/ppermute | solution.py:16
  202.2 4.6 %collective-permute-start.1 = (bf16[1,8,3,4096]{3,2,1,0:T(4,128)(2,1)S(1)}, bf16[1,8,3,4096]{3,2,1,0:T(4,128)(2,1)S(1)}, u32[]{:S(2)}, u32[]{:S(2)}) collective-permute-start(bf16[1,8,3,4096]{3,2,1,0:T(4,128)(2,1)S(1)} %collective-permute-done), channel_id=1, source_target_pairs={{0,30},{2,0},{4,2},{6,4},{8,6},{10,8},{12,10},{14,12},{16,14},{18,... | collective-permute-start | bytes 589832 | tf_op jit(solution)/shard_map/ppermute | solution.py:16
Sparse Core Ops, SparseCore 0:
  357.1 60.6 reduce-scatter.1
where the time goes:
time: 428 us
  other arithmetic  188 us (44%)
  blocking collectives  110 us (26%)
  waiting for transfers between devices  64.7 us (15%)
  local copies, waits for them, and re-layouts  23.7 us (6%)
  matrix products  21.9 us (5%)
  between operations  13.6 us (3%)
  starting transfers between devices  6.33 us (1%)
    another operation x4, other arithmetic  177 us
    all_to_all x1, blocking collectives, shards(): lax.all_to_all(outgoing, 'sens', split_axis=0, concat_axis=0, tiled=True)  110 us
    reduce_scatter x1, waiting for transfers between devices, shards(): lax.psum_scatter(received, 'hour', scatter_dimension=1, tiled=True)  60.8 us
    dot_general x1, matrix products, whiten(): spec = jnp.dot(rows, fwd, preferred_element_type=jnp.float32)  12.1 us
    dot_general x1, matrix products, shards(): jnp.dot(cross.reshape(hours_here * pairs_here * COMPS * COMPS, 2 * NB), i...  9.83 us
  transfers between devices with their start and end apart: 3, of which 2 were waited for; matrix products, arithmetic and copies ran while one was open for 10% of the time, Pallas kernels for 0%

commit v1 on v0

v1 whole, which is shorter than its diff:
```python
import jax
import jax.numpy as jnp
import ml_dtypes
import numpy as np
from jax import lax
from jax.sharding import PartitionSpec as P

SAMPLES = 4096
PADDED = 8192
NB = 2048
LAGS = 1024
COMPS = 3
WIDTH = COMPS * COMPS * LAGS
HALF = SAMPLES // 2


def host_tables():
    times = np.arange(HALF, dtype=np.int64)
    bins = np.arange(NB, dtype=np.int64) + 1
    angle = (times[:, None] * bins[None, :] % PADDED) * (2.0 * np.pi / PADDED)
    fwd = np.concatenate([np.cos(angle), -np.sin(angle)], axis=1).astype(ml_dtypes.bfloat16)
    shifts = np.arange(LAGS, dtype=np.int64) - LAGS // 2
    back = (bins[:, None] * shifts[None, :] % PADDED) * (2.0 * np.pi / PADDED)
    inv = np.concatenate([np.cos(back), -np.sin(back)], axis=0).astype(ml_dtypes.bfloat16)
    return fwd, inv


def whiten(rows, fwd):
    count = rows.shape[0]
    both = jnp.concatenate([rows[:, :HALF], rows[:, HALF:]], axis=0)
    spec = jnp.dot(both, fwd, preferred_element_type=jnp.float32)
    ar, ai = spec[:count, :NB], spec[:count, NB:]
    br, bi = spec[count:, :NB], spec[count:, NB:]
    turn = (lax.broadcasted_iota(jnp.int32, (1, NB), 1) + 1) % 4
    even = turn % 2 == 0
    sign_re = jnp.where((turn == 0) | (turn == 1), 1.0, -1.0)
    sign_im = jnp.where((turn == 0) | (turn == 3), 1.0, -1.0)
    real_part = ar + sign_re * jnp.where(even, br, bi)
    imag_part = ai + sign_im * jnp.where(even, bi, br)
    power = real_part * real_part + imag_part * imag_part
    level = jnp.mean(power, axis=1, keepdims=True)
    scale = 1.0 / jnp.sqrt(power + 0.1 * level + 1e-06)
    return jnp.concatenate([real_part * scale, imag_part * scale], axis=1).astype(jnp.bfloat16)


def from_behind(value, axis, steps):
    count = lax.axis_size(axis)
    pairs = [(source, (source + steps) % count) for source in range(count)]
    return lax.ppermute(value, axis, pairs)


def pick(rows, index):
    table = (index[:, None] == jnp.arange(rows.shape[0], dtype=jnp.int32)[None, :]).astype(jnp.bfloat16)
    return jnp.dot(table, rows, preferred_element_type=jnp.float32)


def shards(windows, pair_first, pair_second, owners):
    hours_here, sensors, _, _ = windows.shape
    pairs = pair_first.shape[0]
    hour_count = lax.axis_size("hour")
    owner_count = lax.axis_size("sens")
    hours = hours_here * hour_count
    columns = WIDTH // hour_count
    capacity = max(2, 2 * pairs // owner_count)
    fwd, inv = (jnp.asarray(table) for table in host_tables())

    white = whiten(windows.reshape(hours_here * sensors * COMPS, SAMPLES), fwd)
    white = lax.all_gather(white, "hour", axis=0, tiled=True)
    white = white.reshape(hours, sensors, COMPS * 2 * NB)
    nearer = from_behind(white, "sens", -1)
    farther = from_behind(white, "sens", -2)
    candidates = jnp.concatenate([white, nearer, farther], axis=1)

    start = lax.axis_index("hour") * columns
    first_block = start // LAGS
    blocks = min(COMPS * COMPS, max((h * columns + columns - 1) // LAGS - h * columns // LAGS + 1 for h in range(hour_count)))
    first_block = jnp.minimum(first_block, COMPS * COMPS - blocks)
    kinds = first_block + jnp.arange(blocks, dtype=jnp.int32)

    total_re, total_im = 0.0, 0.0
    for hour in range(hours):
        a = pick(white[hour], pair_first).reshape(pairs, COMPS, 2, NB)
        b = pick(candidates[hour], pair_second).reshape(pairs, COMPS, 2, NB)
        a = jnp.take(a, kinds // COMPS, axis=1)
        b = jnp.take(b, kinds % COMPS, axis=1)
        ar, ai, br, bi = a[:, :, 0], a[:, :, 1], b[:, :, 0], b[:, :, 1]
        total_re = total_re + (ar * br + ai * bi)
        total_im = total_im + (ar * bi - ai * br)
    cross = jnp.concatenate([total_re, total_im], axis=-1).astype(jnp.bfloat16)
    lagged = jnp.dot(cross.reshape(pairs * blocks, 2 * NB), inv, preferred_element_type=jnp.float32)
    lagged = lagged.astype(jnp.bfloat16).reshape(pairs, blocks * LAGS)
    lagged = lax.dynamic_slice_in_dim(lagged, start - first_block * LAGS, columns, axis=1)

    owner = owners[:, 0]
    order = jnp.arange(pairs, dtype=jnp.int32)
    earlier = (owner[:, None] == owner[None, :]) & (order[None, :] < order[:, None])
    target = owner * capacity + jnp.sum(earlier.astype(jnp.int32), axis=1)
    place = (jnp.arange(owner_count * capacity, dtype=jnp.int32)[:, None] == target[None, :]).astype(jnp.bfloat16)
    outgoing = jnp.dot(place, lagged, preferred_element_type=jnp.float32).astype(jnp.bfloat16)
    received = lax.all_to_all(outgoing, "sens", split_axis=0, concat_axis=0, tiled=True)
    return received.astype(jnp.float32) / jnp.sqrt(jnp.float32(NB * hours))


def solution(mesh):
    placed = (P("hour", "sens", None, None), P("sens"), P("sens"), P("sens", None))
    return jax.shard_map(
        shards, mesh=mesh, in_specs=placed, out_specs=P("sens", "hour"), check_vma=False
    )
```

time: 428 us -> 123 us (0.29)
  other arithmetic: 188 us -> 29 us
  blocking collectives: 110 us -> 40.6 us
  waiting for transfers between devices: 64.7 us -> 0.01 us
  between operations: 13.6 us -> 0.32 us
    another operation x4 -> x2, other arithmetic: 177 us -> 5.59 us
    all_to_all x1, blocking collectives: 110 us -> 32 us  [shards(): lax.all_to_all(outgoing, 'sens', split_axis=0, concat_axis=0, tiled=True)]
    reduce_scatter x1 -> x0, waiting for transfers between devices: 60.8 us -> none  [shards(): lax.psum_scatter(received, 'hour', scatter_dimension=1, tiled=True)]
    select_n x5 -> x4, other arithmetic: 3.46 us -> 21.3 us  [the longest x2 10.9 us: shards(): b = jnp.take(b, kinds % COMPS, axis=1)]
    gather x2 -> x4, local copies, waits for them, and re-layouts: 4.73 us -> 16.6 us  [the longest x2 8.35 us: shards(): b = jnp.take(b, kinds % COMPS, axis=1)]
    all_gather x0 -> x1, blocking collectives: none -> 8.54 us  [shards(): white = lax.all_gather(white, 'hour', axis=0, tiled=True)]
    scatter x1 -> x0, local copies, waits for them, and re-layouts: 5.4 us -> none  [shards(): jnp.zeros((owner_count * capacity, width), jnp.float32).at[target]]
    add x1 -> x2, local copies, waits for them, and re-layouts: 6.72 us -> 1.99 us  [the longest x1 1.41 us: shards(): total_im = total_im + (ar * bi - ai * br)]
  transfers between devices with their start and end apart: 3 -> 2, of which waited for: 2 -> 0; matrix products, arithmetic and copies ran while one was open for 10% -> 20% of each run, Pallas kernels for 0% -> 0%
where the time goes in v1:
time: 123 us
  blocking collectives  40.6 us (33%)
  other arithmetic  29 us (24%)
  local copies, waits for them, and re-layouts  27.7 us (23%)
  matrix products  20.6 us (17%)
  starting transfers between devices  4.82 us (4%)
    all_to_all x1, blocking collectives, shards(): lax.all_to_all(outgoing, 'sens', split_axis=0, concat_axis=0, tiled=True)  32 us
    select_n x2, other arithmetic, shards(): b = jnp.take(b, kinds % COMPS, axis=1)  10.9 us
    select_n x1, other arithmetic, shards(): a = jnp.take(a, kinds // COMPS, axis=1)  10.3 us
    dot_general x1, matrix products, whiten(): spec = jnp.dot(both, fwd, preferred_element_type=jnp.float32)  8.8 us
    all_gather x1, blocking collectives, shards(): white = lax.all_gather(white, 'hour', axis=0, tiled=True)  8.54 us
    gather x2, local copies, waits for them, and re-layouts, shards(): b = jnp.take(b, kinds % COMPS, axis=1)  8.35 us
    gather x2, local copies, waits for them, and re-layouts, shards(): a = jnp.take(a, kinds // COMPS, axis=1)  8.28 us
    dot_general x4, matrix products, pick(): return jnp.dot(table, rows, preferred_element_type=jnp.float32)  5.92 us
  transfers between devices with their start and end apart: 2, of which 0 were waited for; matrix products, arithmetic and copies ran while one was open for 20% of the time, Pallas kernels for 0%

profile of v1, /device:TPU:0, one launch (start us, length us, event | category | flops | bytes accessed | tf_op | source)
XLA Modules:
  0.0 123.0 jit_solution(4290551004655032811)
XLA Ops:
  0.0 1.1 copy.12
  1.1 0.2 reshape.138
  1.3 8.8 %fusion.7 = f32[48,4096]{1,0:T(8,128)S(1)} fusion(bf16[2048,4096]{1,0:T(8,128)(2,1)} %constant.107.clone, bf16[24,2048]{1,0:T(8,128)(2,1)S(1)} %get-tuple-element.18, bf16[24,2048]{1,0:T(8,128)(2,1)S(1)} %get-tuple-element.17), kind=kOutput, calls=%fused_computation.30 | convolution fusion | flops 805699584 | bytes 17760256 | tf_op jit(solution)/shard_map/dot_general | solution.py:31
  10.1 0.2 fusion.8
  10.3 0.1 multiply_convert_fusion.1
  10.5 8.5 %all_gather.3 = bf16[48,4096]{1,0:T(8,128)(2,1)S(1)} all-gather(bf16[24,4096]{1,0:T(8,128)(2,1)S(1)} %pad_maximum_fusion.1), channel_id=1, replica_groups=mesh['sens'=16,'hour'=2] {'hour'}, dimensions={0}, use_global_device_ids=true | all-gather | bytes 589824 | tf_op jit(solution)/shard_map/all_gather | solution.py:68
  19.0 0.2 reshape.139
  19.2 4.8 %collective-permute-start.1 = (bf16[2,8,12288]{2,1,0:T(8,128)(2,1)S(1)}, bf16[2,8,12288]{2,1,0:T(8,128)(2,1)}, u32[]{:S(2)}, u32[]{:S(2)}) collective-permute-start(bf16[2,8,12288]{2,1,0:T(8,128)(2,1)S(1)} %reshape.139), channel_id=1, source_target_pairs={{0,28},{2,30},{4,0},{6,2},{8,4},{10,6},{12,8},{14,10},{16,12},{18,... | collective-permute-start | bytes 1179656 | tf_op jit(solution)/shard_map/ppermute | solution.py:49
  24.1 0.0 collective-permute-start
  24.1 0.6 compare_select_fusion
  24.7 0.8 constant_dynamic-update-slice_fusion.2
  25.5 0.8 squeeze.11
  26.3 0.1 squeeze.26
  26.4 2.3 %fusion.23 = f32[64,3,2,2048]{3,0,2,1:T(8,128)} fusion(bf16[3,2,2048,8]{2,3,1,0:T(8,128)(2,1)S(1)} %bitcast.60, s32[64]{0:T(128)S(1)} %copy-done.4), kind=kOutput, calls=%fused_computation.63 | convolution fusion | flops 12583424 | bytes 3342592 | tf_op jit(solution)/shard_map/dot_general | solution.py:54
  28.7 0.6 fusion.25
  29.3 5.1 %gather_fusion.2 = f32[5,64,2,2048]{3,1,2,0:T(8,128)} fusion(f32[64,3,2,2048]{3,0,2,1:T(8,128)} %fusion.23, s32[1024]{0:T(1024)S(1)} %pad_clamp_fusion.1), kind=kCustom, calls=%fused_computation.2.clone | custom fusion | bytes 10485780 | tf_op jit(solution)/shard_map/jit(_take)/gather | solution.py:84
  34.5 3.1 %gather_fusion = f32[5,64,2,2048]{3,1,2,0:T(8,128)} fusion(f32[64,3,2,2048]{3,0,2,1:T(8,128)S(1)} %fusion.25, s32[1024]{0:T(1024)S(1)} %pad_clamp_fusion.1), kind=kCustom, calls=%fused_computation.clone | custom fusion | bytes 10485780 | tf_op jit(solution)/shard_map/jit(_take)/gather | solution.py:84
  37.6 10.3 %select_bitcast_fusion.3 = (f32[64,5,2,2048]{3,0,2,1:T(8,128)}, f32[64,5,2,2048]{3,0,2,1:T(8,128)}) fusion(f32[5,64,2,2048]{3,1,2,0:T(8,128)} %gather_fusion, pred[5]{0:T(512)(128)(4,1)S(1)} %get-tuple-element.28, f32[5,64,2,2048]{3,1,2,0:T(8,128)} %gather_fusion.2), kind=kLoop, calls=%fused_computation.9 | loop fusion | flops 2621440 | bytes 20971524 | tf_op jit(solution)/shard_map/jit(_take)/select_n | solution.py:84
  47.9 0.0 copy-done.6
  48.0 0.2 convert_reduce_fusion
  48.2 0.0 collective-permute-done
  48.2 1.0 constant_dynamic-update-slice_fusion.1
  49.2 0.0 copy-start.5
  49.2 0.0 collective-permute-done.1
  49.2 1.0 constant_dynamic-update-slice_fusion
  50.3 0.1 slice_bitcast_fusion.1
  50.4 1.2 %dot_general.42 = bf16[3,2,2048,24]{2,1,0,3:T(2,128)(2,1)} reshape(bf16[12288,24]{0,1:T(8,128)(2,1)S(1)} %get-tuple-element.11) | data formatting | bytes 1179648 | tf_op jit(solution)/shard_map/dot_general | solution.py:54
  51.6 0.4 dot_general.48
  52.0 0.0 copy-start
  52.0 2.4 %fusion.2 = f32[64,3,2,2048]{3,0,2,1:T(8,128)} fusion(bf16[3,2,2048,24]{2,1,0,3:T(2,128)(2,1)S(1)} %dot_general.48, s32[64]{0:T(128)S(1)} %copy-done.5), kind=kOutput, calls=%fused_computation.17 | convolution fusion | flops 37750272 | bytes 3735808 | tf_op jit(solution)/shard_map/dot_general | solution.py:54
  54.5 0.0 copy-done
  54.5 0.6 fusion.4
  55.1 5.1 %gather_fusion.3 = f32[5,64,2,2048]{3,1,2,0:T(8,128)} fusion(f32[64,3,2,2048]{3,0,2,1:T(8,128)} %fusion.2, s32[1024]{0:T(1024)S(1)} %pad_clamp_fusion), kind=kCustom, calls=%fused_computation.3.clone | custom fusion | bytes 10485780 | tf_op jit(solution)/shard_map/jit(_take)/gather | solution.py:85
  60.2 3.2 %gather_fusion.1 = f32[5,64,2,2048]{3,1,2,0:T(8,128)} fusion(f32[64,3,2,2048]{3,0,2,1:T(8,128)S(1)} %fusion.4, s32[1024]{0:T(1024)S(1)} %pad_clamp_fusion), kind=kCustom, calls=%fused_computation.1.clone | custom fusion | bytes 10485780 | tf_op jit(solution)/shard_map/jit(_take)/gather | solution.py:85
  63.5 10.4 %select_bitcast_fusion.2 = (f32[64,5,2,2048]{3,0,2,1:T(8,128)}, f32[64,5,2,2048]{3,0,2,1:T(8,128)}) fusion(f32[5,64,2,2048]{3,1,2,0:T(8,128)} %gather_fusion.1, pred[5]{0:T(512)(128)(4,1)S(1)} %get-tuple-element.27, f32[5,64,2,2048]{3,1,2,0:T(8,128)} %gather_fusion.3), kind=kLoop, calls=%fused_computation.8 | loop fusion | flops 2621440 | bytes 20971524 | tf_op jit(solution)/shard_map/jit(_take)/select_n | solution.py:85
  73.9 5.5 %add_convert_fusion = (bf16[64,5,1,2048]{3,0,2,1:T(8,128)(2,1)S(1)}, bf16[64,5,1,2048]{3,0,2,1:T(8,128)(2,1)S(1)}) fusion(f32[64,5,2,2048]{3,0,2,1:T(8,128)} %get-tuple-element.22, f32[64,5,2,2048]{3,0,2,1:T(8,128)S(1)} %bitcast.58, f32[64,5,2,2048]{3,0,2,1:T(8,128)} %get-tuple-element.21, f32[64,5,2,2048]{3,0,2,1:T(8,128)S(1)} %bitcast.56), kind=kLoop, calls=%fused_computation.10 | loop fusion | flops 10485760 | bytes 23592960 | tf_op jit(solution)/shard_map/convert.2
  79.3 0.7 copy.16
  80.1 1.4 %add.149 = bf16[320,2048]{1,0:T(8,128)(2,1)} reshape(bf16[64,5,1,2048]{3,1,0,2:T(8,128)(2,1)S(1)} %copy.16) | data formatting | bytes 2621440 | tf_op jit(solution)/shard_map/add | solution.py:88
  81.5 0.7 copy.15
  82.3 0.6 add.147
  82.8 0.0 copy-start.2
  82.9 0.0 copy-start.8
  82.9 3.9 %fusion.34 = f32[320,1024]{1,0:T(8,128)S(1)} fusion(bf16[320,2048]{1,0:T(8,128)(2,1)S(1)} %add.147, bf16[2048,1024]{1,0:T(8,128)(2,1)} %constant.110), kind=kOutput, calls=%fused_computation.81 | convolution fusion | flops 1342177280 | bytes 6815744 | tf_op jit(solution)/shard_map/dot_general | solution.py:90
  86.8 1.5 %fusion.1 = bf16[320,1024]{1,0:T(8,128)(2,1)S(1)} fusion(f32[320,1024]{1,0:T(8,128)S(1)} %fusion.34, bf16[320,2048]{1,0:T(8,128)(2,1)S(1)} %copy-done.2, bf16[2048,1024]{1,0:T(8,128)(2,1)S(1)} %copy-done.8), kind=kOutput, calls=%fused_computation.14 | convolution fusion | flops 1342832640 | bytes 7471104 | tf_op jit(solution)/shard_map/dot_general | solution.py:90
  88.3 0.5 reshape.140
  88.8 0.5 fusion
  89.3 32.0 %all_to_all.9 = bf16[16,8,4608]{2,1,0:T(8,128)(2,1)S(1)} all-to-all(bf16[16,8,4608]{2,1,0:T(8,128)(2,1)S(1)} %fusion), channel_id=1, replica_groups=mesh['sens'=16,'hour'=2] {'sens'}, dimensions={0} | all-to-all | bytes 2359296 | tf_op jit(solution)/shard_map/all_to_all | solution.py:100
  121.3 1.6 %multiply_bitcast_fusion = f32[128,4608]{1,0:T(8,128)} fusion(bf16[16,8,4608]{2,1,0:T(8,128)(2,1)S(1)} %all_to_all.9), kind=kLoop, calls=%fused_computation.12 | loop fusion | flops 1179648 | bytes 3538944 | tf_op jit(solution)/shard_map/div | solution.py:101
  (32 shorter events, 0.2 us)
Async XLA Ops:
  10.3 16.1 %copy-start.4 = (s32[64]{0:T(128)S(1)}, s32[64]{0:T(128)}, u32[]{:S(2)}) copy-start(s32[64]{0:T(128)} %param.9) | copy-start | bytes 772
  19.2 30.0 %collective-permute-start.1 = (bf16[2,8,12288]{2,1,0:T(8,128)(2,1)S(1)}, bf16[2,8,12288]{2,1,0:T(8,128)(2,1)}, u32[]{:S(2)}, u32[]{:S(2)}) collective-permute-start(bf16[2,8,12288]{2,1,0:T(8,128)(2,1)S(1)} %reshape.139), channel_id=1, source_target_pairs={{0,28},{2,30},{4,0},{6,2},{8,4},{10,6},{12,8},{14,10},{16,12},{18,... | collective-permute-start | bytes 1179656 | tf_op jit(solution)/shard_map/ppermute | solution.py:49
  24.1 24.1 %collective-permute-start = (bf16[2,8,12288]{2,1,0:T(8,128)(2,1)S(1)}, bf16[2,8,12288]{2,1,0:T(8,128)(2,1)}, u32[]{:S(2)}, u32[]{:S(2)}) collective-permute-start(bf16[2,8,12288]{2,1,0:T(8,128)(2,1)S(1)} %reshape.139), channel_id=1, source_target_pairs={{0,30},{2,0},{4,2},{6,4},{8,6},{10,8},{12,10},{14,12},{16,14},{18,... | collective-permute-start | bytes 1179656 | tf_op jit(solution)/shard_map/ppermute | solution.py:49
  26.4 2.3 %copy-start.3 = (bf16[8,12288]{1,0:T(8,128)(2,1)S(1)}, bf16[8,12288]{1,0:T(8,128)(2,1)}, u32[]{:S(2)}) copy-start(bf16[8,12288]{1,0:T(8,128)(2,1)} %squeeze.11) | copy-start | bytes 589828
  37.6 10.3 %copy-start.6 = (s32[5]{0:T(128)S(1)}, s32[5]{0:T(128)}, u32[]{:S(2)}) copy-start(s32[5]{0:T(128)} %get-tuple-element.25) | copy-start | bytes 64
  37.6 10.4 %copy-start.7 = (s32[64,1]{0,1:T(1,128)S(1)}, s32[64,1]{0,1:T(1,128)}, u32[]{:S(2)}) copy-start(s32[64,1]{0,1:T(1,128)} %param.11) | copy-start | bytes 772
  37.6 10.6 %copy-start.1 = (bf16[2,24,12288]{2,1,0:T(8,128)(2,1)S(1)}, bf16[2,24,12288]{2,1,0:T(8,128)(2,1)}, u32[]{:S(2)}) copy-start(bf16[2,24,12288]{2,1,0:T(8,128)(2,1)} %constant_dynamic-update-slice_fusion.2) | copy-start | bytes 3538948
  49.2 2.8 %copy-start.5 = (s32[64]{0:T(128)S(1)}, s32[64]{0:T(128)}, u32[]{:S(2)}) copy-start(s32[64]{0:T(128)} %param.10) | copy-start | bytes 772
  52.0 2.4 %copy-start = (bf16[3,2,2048,24]{2,1,0,3:T(2,128)(2,1)S(1)}, bf16[3,2,2048,24]{2,1,0,3:T(2,128)(2,1)}, u32[]{:S(2)}) copy-start(bf16[3,2,2048,24]{2,1,0,3:T(2,128)(2,1)} %dot_general.42) | copy-start | bytes 1769476
  63.5 10.4 %slice-start = ((s8[5242880]{0:T(1024)(128)(4,1)}), s8[4194304]{0:T(1024)(128)(4,1)S(1)}, s32[]{:S(2)}) async-start(s8[5242880]{0:T(1024)(128)(4,1)} %bitcast.55), calls=%async_computation.1 | async-start | bytes 8388608
  63.5 10.4 %slice-start.2 = ((s8[5242880]{0:T(1024)(128)(4,1)}), s8[4194304]{0:T(1024)(128)(4,1)S(1)}, s32[]{:S(2)}) async-start(s8[5242880]{0:T(1024)(128)(4,1)} %bitcast.57), calls=%async_computation.3 | async-start | bytes 8388608
  63.5 10.4 %slice-start.1 = ((s8[5242880]{0:T(1024)(128)(4,1)}), s8[1048576]{0:T(1024)(128)(4,1)S(1)}, s32[]{:S(2)}) async-start(s8[5242880]{0:T(1024)(128)(4,1)} %bitcast.55), calls=%async_computation.2 | async-start | bytes 2097152
  63.5 10.4 %slice-start.3 = ((s8[5242880]{0:T(1024)(128)(4,1)}), s8[1048576]{0:T(1024)(128)(4,1)S(1)}, s32[]{:S(2)}) async-start(s8[5242880]{0:T(1024)(128)(4,1)} %bitcast.57), calls=%async_computation.4 | async-start | bytes 2097152
  82.8 3.9 %copy-start.2 = (bf16[320,2048]{1,0:T(8,128)(2,1)S(1)}, bf16[320,2048]{1,0:T(8,128)(2,1)}, u32[]{:S(2)}) copy-start(bf16[320,2048]{1,0:T(8,128)(2,1)} %add.149) | copy-start | bytes 3932164
  82.9 3.9 %copy-start.8 = (bf16[2048,1024]{1,0:T(8,128)(2,1)S(1)}, bf16[2048,1024]{1,0:T(8,128)(2,1)}, u32[]{:S(2)}) copy-start(bf16[2048,1024]{1,0:T(8,128)(2,1)} %constant.111) | copy-start | bytes 12582916

commit v2 on v1

--- a/solution.py
+++ b/solution.py
@@ -1,8 +1,12 @@
+import functools
+
 import jax
 import jax.numpy as jnp
 import ml_dtypes
 import numpy as np
 from jax import lax
+from jax.experimental import pallas as pl
+from jax.experimental.pallas import tpu as pltpu
 from jax.sharding import PartitionSpec as P
 
 SAMPLES = 4096
@@ -12,7 +16,12 @@
 COMPS = 3
 WIDTH = COMPS * COMPS * LAGS
 HALF = SAMPLES // 2
-
+QUARTER = NB // 2
+BLOCK = 128
+CHUNKS = QUARTER // BLOCK
+MESH = pl.DeviceIdType.MESH
+F32 = jnp.float32
+BF16 = jnp.bfloat16
 
 def host_tables():
     times = np.arange(HALF, dtype=np.int64)
@@ -54,7 +63,7 @@
     return jnp.dot(table, rows, preferred_element_type=jnp.float32)
 
 
-def shards(windows, pair_first, pair_second, owners):
+def plain_shards(windows, pair_first, pair_second, owners):
     hours_here, sensors, _, _ = windows.shape
     pairs = pair_first.shape[0]
     hour_count = lax.axis_size("hour")
@@ -101,8 +110,300 @@
     return received.astype(jnp.float32) / jnp.sqrt(jnp.float32(NB * hours))
 
 
+def folded_tables():
+    times = np.arange(HALF, dtype=np.int64)
+    bins = np.arange(QUARTER, dtype=np.int64)
+    angle = (times[:, None] * bins[None, :] % PADDED) * (2.0 * np.pi / PADDED)
+    cosine, sine = np.cos(angle), np.sin(angle)
+    sine[:, 0] = 1 - 2 * (times // 4 % 2)
+    both = np.stack([cosine.reshape(HALF, CHUNKS, BLOCK), sine.reshape(HALF, CHUNKS, BLOCK)], axis=2)
+    fwd = both.transpose(1, 0, 2, 3).reshape(CHUNKS, HALF, 2 * BLOCK).astype(ml_dtypes.bfloat16)
+    order = np.concatenate([bins, NB - bins])
+    order[0] = QUARTER
+    shifts = np.arange(LAGS, dtype=np.int64) - LAGS // 2
+    back = (order[:, None] * shifts[None, :] % PADDED) * (2.0 * np.pi / PADDED)
+    inv = np.concatenate([np.cos(back), -np.sin(back)], axis=0)
+    inv = inv.reshape(2 * NB, 4, LAGS // 4).transpose(1, 0, 2).astype(ml_dtypes.bfloat16)
+    return fwd, inv
+
+
+def kernel(
+    n, pairs, x_ref, first_ref, second_ref, owner_col_ref, owner_row_ref, fwd_hbm, inv_hbm, out_ref,
+    fwd_v, inv_v, xm, spec, white, a_v, b_v, cross, lagged, outgoing,
+    fwd_sem, inv_sem, near_send, near_recv, far_send, far_recv, own_sem,
+):
+    me = lax.axis_index("sens")
+    hour = lax.axis_index("hour")
+    other = 1 - hour
+
+    barrier = pltpu.get_barrier_semaphore()
+
+    def greet(step, carry):
+        pl.semaphore_signal(barrier, inc=1, device_id=(lax.rem(me + step, n), hour), device_id_type=MESH)
+        return carry
+
+    lax.fori_loop(1, n, greet, 0)
+    pl.semaphore_signal(barrier, inc=1, device_id=(me, other), device_id_type=MESH)
+
+    def fwd_copy(c):
+        return pltpu.make_async_copy(fwd_hbm.at[c], fwd_v.at[c], fwd_sem.at[c])
+
+    def inv_copy(c):
+        return pltpu.make_async_copy(inv_hbm.at[c], inv_v.at[c], inv_sem.at[c])
+
+    for c in range(CHUNKS):
+        fwd_copy(c).start()
+    for c in range(4):
+        inv_copy(c).start()
+
+    rows = x_ref.shape[0]
+    x = x_ref[...].astype(F32)
+    halves = jnp.concatenate([x[:, :HALF], x[:, HALF:]], axis=0)
+    residue = lax.broadcasted_iota(jnp.int32, (2 * rows, HALF), 1) & 3
+    xm[...] = jnp.concatenate([jnp.where(residue == r, halves, 0.0) for r in range(4)], axis=0).astype(BF16)
+
+    lane = lax.broadcasted_iota(jnp.int32, (rows, BLOCK), 1)
+    turn = lane & 3
+    root = 0.70703125
+
+    def transform(c, total):
+        fwd_copy(c).wait()
+        part = jnp.dot(xm[...], fwd_v[c], preferred_element_type=F32)
+        pc, ps = [], []
+        for r in range(4):
+            top = part[2 * r * rows:(2 * r + 1) * rows]
+            low = part[(2 * r + 1) * rows:(2 * r + 2) * rows]
+            c1, s1 = low[:, :BLOCK], low[:, BLOCK:]
+            pc.append(top[:, :BLOCK] + jnp.where(turn == 0, c1, jnp.where(turn == 1, -s1, jnp.where(turn == 2, -c1, s1))))
+            ps.append(top[:, BLOCK:] + jnp.where(turn == 0, s1, jnp.where(turn == 1, c1, jnp.where(turn == 2, -s1, -c1))))
+        ends = (lane == 0) & (c == 0)
+        re_a = jnp.where(ends, ps[0] + root * (ps[1] - ps[3]), pc[0] + pc[1] + pc[2] + pc[3])
+        im_a = -jnp.where(ends, ps[2] + root * (ps[1] + ps[3]), ps[0] + ps[1] + ps[2] + ps[3])
+        zero_sine = jnp.where(ends, 0.0, 1.0)
+        re_b = pc[0] - pc[2] + zero_sine * (ps[1] - ps[3])
+        im_b = pc[3] - pc[1] + zero_sine * (ps[0] - ps[2])
+        near = pl.ds(pl.multiple_of(c * BLOCK, BLOCK), BLOCK)
+        far = pl.ds(pl.multiple_of(QUARTER + c * BLOCK, BLOCK), BLOCK)
+        spec[0, :, near] = re_a
+        spec[0, :, far] = re_b
+        spec[1, :, near] = im_a
+        spec[1, :, far] = im_b
+        return total + (re_a * re_a + im_a * im_a) + (re_b * re_b + im_b * im_b)
+
+    total = lax.fori_loop(0, CHUNKS, transform, jnp.zeros((rows, BLOCK), F32))
+    level = jnp.sum(total, axis=1, keepdims=True) * (1.0 / NB)
+    real_part, imag_part = spec[0], spec[1]
+    scale = 1.0 / jnp.sqrt(real_part * real_part + imag_part * imag_part + 0.1 * level + 1e-06)
+    white[0, 0] = jnp.concatenate([real_part * scale, imag_part * scale], axis=0).astype(BF16)
+
+    pl.semaphore_wait(barrier, n)
+    even = lax.rem(me, 2) == 0
+    odd = lax.rem(me, 2) == 1
+    behind = (lax.rem(me + n - 1, n), hour)
+    behind2 = (lax.rem(me + n - 2, n), hour)
+    ahead = (lax.rem(me + 1, n), hour)
+    across = (me, other)
+
+    def near_copy(src, dst, send, recv, device):
+        return pltpu.make_async_remote_copy(
+            src_ref=white.at[src[0], src[1]], dst_ref=white.at[dst[0], dst[1]],
+            send_sem=near_send.at[send], recv_sem=near_recv.at[recv], device_id=device, device_id_type=MESH,
+        )
+
+    copy_far = near_copy((0, 0), (0, 2), 0, 0, behind2)
+    copy_hour = near_copy((0, 0), (1, 0), 1, 1, across)
+    copy_both = near_copy((0, 2), (1, 2), 2, 2, across)
+    odd_own = near_copy((0, 0), (0, 1), 3, 3, behind)
+    even_own = near_copy((0, 2), (0, 1), 3, 3, ahead)
+    odd_other = near_copy((1, 0), (1, 1), 4, 4, behind)
+    even_other = near_copy((1, 2), (1, 1), 4, 4, ahead)
+
+    copy_far.start()
+    copy_hour.start()
+
+    @pl.when(odd)
+    def _():
+        odd_own.start()
+
+    copy_far.wait_recv()
+    copy_both.start()
+
+    @pl.when(even)
+    def _():
+        even_own.start()
+
+    copy_hour.wait_recv()
+
+    @pl.when(odd)
+    def _():
+        odd_other.start()
+
+    half_rows = rows
+    group = 2 * rows
+    wide = lax.broadcasted_iota(jnp.int32, (pairs, 3 * group), 1)
+    first, second = first_ref[...], second_ref[...]
+    second_base = second // 8 * group + second % 8 * COMPS
+    pick_a, pick_b = [], []
+    for part in range(2):
+        for comp in range(COMPS):
+            shift = part * half_rows + comp
+            pick_a.append(jnp.where(wide[:, :group] == first * COMPS + shift, 1.0, 0.0))
+            pick_b.append(jnp.where(wide == second_base + shift, 1.0, 0.0))
+    pick_a = jnp.concatenate(pick_a, axis=0).astype(BF16)
+    pick_b = jnp.concatenate(pick_b, axis=0).astype(BF16)
+    order_col = lax.broadcasted_iota(jnp.int32, (pairs, 2 * pairs), 0)
+    order_row = lax.broadcasted_iota(jnp.int32, (pairs, 2 * pairs), 1) % pairs
+    owner_row = owner_row_ref[...]
+    earlier = (owner_col_ref[...] == owner_row) & (order_col < order_row)
+    slot = jnp.sum(jnp.where(earlier, 1, 0), axis=0, keepdims=True)
+    side = lax.broadcasted_iota(jnp.int32, (1, 2 * pairs), 1) // pairs
+    target = owner_row * 16 + side * 8 + slot
+    place = jnp.where(lax.broadcasted_iota(jnp.int32, (16 * n, 2 * pairs), 0) == target, 1.0, 0.0).astype(BF16)
+
+    copy_both.wait_recv()
+
+    @pl.when(even)
+    def _():
+        even_other.start()
+
+    odd_own.wait_recv()
+    odd_other.wait_recv()
+
+    step = 256
+
+    def correlate(q, carry):
+        lanes = pl.ds(pl.multiple_of(q * step, step), step)
+        for h in range(2):
+            a_v[h] = jnp.dot(pick_a, white[h, 0, :, lanes], preferred_element_type=F32).reshape(2, COMPS, pairs, step)
+            b_v[h] = jnp.dot(
+                pick_b, white[h, :, :, lanes].reshape(3 * group, step), preferred_element_type=F32
+            ).reshape(2, COMPS, pairs, step)
+        for i in range(5):
+            kind = hour * 4 + i
+            c, e = kind // COMPS, kind % COMPS
+            re, im = 0.0, 0.0
+            for h in range(2):
+                ar, ai, br, bi = a_v[h, 0, c], a_v[h, 1, c], b_v[h, 0, e], b_v[h, 1, e]
+                re = re + (ar * br + ai * bi)
+                im = im + (ar * bi - ai * br)
+            cross[pl.ds(i * pairs, pairs), lanes] = re.astype(BF16)
+            cross[pl.ds(i * pairs, pairs), pl.ds(pl.multiple_of(NB + q * step, step), step)] = im.astype(BF16)
+        return carry
+
+    lax.fori_loop(0, NB // step, correlate, 0)
+    for c in range(4):
+        inv_copy(c).wait()
+
+    def far_copy(part, source, dst):
+        count = 5 - part
+        return pltpu.make_async_remote_copy(
+            src_ref=outgoing.at[dst, pl.ds(0, count), part], dst_ref=out_ref.at[source, pl.ds(0, count), part],
+            send_sem=far_send.at[part, dst], recv_sem=far_recv.at[part, source],
+            device_id=(dst, hour), device_id_type=MESH,
+        )
+
+    def own_copy(part):
+        count = 5 - part
+        return pltpu.make_async_copy(
+            outgoing.at[me, pl.ds(0, count), part], out_ref.at[me, pl.ds(0, count), part], own_sem.at[part]
+        )
+
+    for part in range(2):
+        count = 5 - part
+        first_row = pl.multiple_of(part * hour * pairs, pairs)
+        lag_half = hour if part == 0 else other
+        source = cross[pl.ds(first_row, count * pairs), :]
+        for side in range(2):
+            lagged[side, pl.ds(0, count * pairs)] = jnp.dot(
+                source, inv_v[lag_half * 2 + side], preferred_element_type=F32
+            ).astype(BF16)
+        for i in range(count):
+            both = lagged[:, pl.ds(i * pairs, pairs)].reshape(2 * pairs, 256)
+            moved = jnp.dot(place, both, preferred_element_type=F32).astype(BF16)
+            outgoing[:, i, part] = moved.reshape(n, 16, 256)
+
+        def send(step, carry, part=part):
+            far_copy(part, me, lax.rem(me + step, n)).start()
+            return carry
+
+        lax.fori_loop(1, n, send, 0)
+        own_copy(part).start()
+
+    def finish(step, carry):
+        peer = lax.rem(me + step, n)
+        for part in range(2):
+            copy = far_copy(part, peer, peer)
+            copy.wait_send()
+            copy.wait_recv()
+        return carry
+
+    lax.fori_loop(1, n, finish, 0)
+    for part in range(2):
+        own_copy(part).wait()
+    copy_far.wait_send()
+    copy_hour.wait_send()
+    copy_both.wait_send()
+    odd_own.wait_send()
+    odd_other.wait_send()
+
+
+def shards(windows, pair_first, pair_second, owners):
+    n = lax.axis_size("sens")
+    rows = windows.shape[1] * COMPS
+    pairs = pair_first.shape[0]
+    fwd, inv = (jnp.asarray(table) for table in folded_tables())
+    vmem = pl.BlockSpec(memory_space=pltpu.VMEM)
+    anywhere = pl.BlockSpec(memory_space=pl.ANY)
+    received = pl.pallas_call(
+        functools.partial(kernel, n, pairs),
+        out_shape=jax.ShapeDtypeStruct((n, 5, 2, 16, 256), BF16),
+        in_specs=[vmem] * 5 + [anywhere] * 2,
+        out_specs=anywhere,
+        scratch_shapes=[
+            pltpu.VMEM(fwd.shape, BF16),
+            pltpu.VMEM(inv.shape, BF16),
+            pltpu.VMEM((8 * rows, HALF), BF16),
+            pltpu.VMEM((2, rows, NB), F32),
+            pltpu.VMEM((2, 3, 2 * rows, NB), BF16),
+            pltpu.VMEM((2, 2, COMPS, pairs, 256), F32),
+            pltpu.VMEM((2, 2, COMPS, pairs, 256), F32),
+            pltpu.VMEM((5 * pairs, 2 * NB), BF16),
+            pltpu.VMEM((2, 5 * pairs, 256), BF16),
+            pltpu.VMEM((n, 5, 2, 16, 256), BF16),
+            pltpu.SemaphoreType.DMA((CHUNKS,)),
+            pltpu.SemaphoreType.DMA((4,)),
+            pltpu.SemaphoreType.DMA((5,)),
+            pltpu.SemaphoreType.DMA((5,)),
+            pltpu.SemaphoreType.DMA((2, n)),
+            pltpu.SemaphoreType.DMA((2, n)),
+            pltpu.SemaphoreType.DMA((2,)),
+        ],
+        compiler_params=pltpu.CompilerParams(
+            collective_id=0, has_side_effects=True, vmem_limit_bytes=50 * 2**20
+        ),
+    )(
+        windows.reshape(rows, SAMPLES),
+        pair_first[:, None],
+        pair_second[:, None],
+        owners,
+        jnp.tile(owners[:, 0], 2)[None, :],
+        fwd,
+        inv,
+    )
+    received = received.reshape(n, 10, 2, 8, 256)[:, :9].transpose(0, 3, 1, 2, 4).reshape(n * 8, WIDTH // 2)
+    return received.astype(F32) / jnp.sqrt(F32(2 * NB))
+
+
 def solution(mesh):
     placed = (P("hour", "sens", None, None), P("sens"), P("sens"), P("sens", None))
-    return jax.shard_map(
-        shards, mesh=mesh, in_specs=placed, out_specs=P("sens", "hour"), check_vma=False
-    )
+
+    def run(windows, pair_first, pair_second, owners):
+        n, hours = mesh.shape["sens"], mesh.shape["hour"]
+        pairs = pair_first.shape[0] // n
+        fits = hours == 2 and windows.shape[0] == 2 and n == 16 and pairs == 64 and windows.shape[1] == 8 * n
+        body = shards if fits else plain_shards
+        return jax.shard_map(
+            body, mesh=mesh, in_specs=placed, out_specs=P("sens", "hour"), check_vma=False
+        )(windows, pair_first, pair_second, owners)
+
+    return run

time: 123 us -> 60.6 us (0.49)
  the two profiles are of different devices: /device:TPU:0 before, /device:TPU:11 now
where the time goes in v2:
time: 60.6 us; the launch traced here: 60.4 us
  Pallas kernels  54.5 us (90%)
  local copies, waits for them, and re-layouts  4.24 us (7%)
  other arithmetic  1.72 us (3%)
    pallas_call x1, Pallas kernels, shards(): pl.pallas_call(functools.partial(kernel, n, pairs), out_shape=jax.ShapeDt...  54.5 us
    unnamed x2, local copies, waits for them, and re-layouts  1.84 us
    div x1, other arithmetic, shards(): return received.astype(F32) / jnp.sqrt(F32(2 * NB))  1.72 us

profile of v2, /device:TPU:11, one launch (start us, length us, event | category | flops | bytes accessed | tf_op | source)
XLA Modules:
  0.0 60.4 jit_solution(13923251150028231140)
XLA Ops:
  0.0 0.7 %tile.8 = s32[2,64]{1,0:T(2,128)S(1)} broadcast(s32[64]{0:T(128)} %bitcast.10), dimensions={1} | broadcast | bytes 768 | tf_op jit(solution)/shard_map/tile | solution.py:389
  0.7 0.1 broadcast_in_dim_tile.3.owner_row_ref
  0.7 0.7 %copy.12.first_ref = s32[64,1]{1,0:T(8,128)S(1)} copy(s32[64,1]{0,1:T(1,128)} %bitcast.8) | data formatting | bytes 512 | tf_op jit(solution)/shard_map/broadcast_in_dim | solution.py:386
  1.5 0.7 %copy.13.second_ref = s32[64,1]{1,0:T(8,128)S(1)} copy(s32[64,1]{0,1:T(1,128)} %bitcast.9) | data formatting | bytes 512 | tf_op jit(solution)/shard_map/broadcast_in_dim | solution.py:387
  2.2 0.7 %copy.14.owner_col_ref = s32[64,1]{1,0:T(8,128)S(1)} copy(s32[64,1]{0,1:T(1,128)} %param.9) | data formatting | bytes 512 | tf_op args[3]
  3.0 1.1 %copy.11 = bf16[1,8,3,4096]{3,2,1,0:T(4,128)(2,1)S(1)} copy(bf16[1,8,3,4096]{3,1,2,0:T(8,128)(2,1)} %param.6) | data formatting | bytes 393216 | tf_op args[0]
  4.1 0.2 reshape.11.x_ref
  4.2 54.5 %shard_map.64 = bf16[16,5,2,16,256]{4,3,2,1,0:T(8,128)(2,1)S(1)} custom-call(bf16[24,4096]{1,0:T(8,128)(2,1)S(1)} %reshape.11.x_ref, s32[64,1]{1,0:T(8,128)S(1)} %copy.12.first_ref, s32[64,1]{1,0:T(8,128)S(1)} %copy.13.second_ref, s32[64,1]{1,0:T(8,128)S(1)} %copy.14.owner_col_ref, s32[1,128]{1,0:T(1,128)S(1)} %broadcast_in_dim_tile.3.owner_row_ref, ...), custom_call_target="tpu_custom_call" | custom-call | tf_op jit(solution)/shard_map/pallas_call | solution.py:357
  58.7 1.7 %convert_multiply_fusion = f32[16,9,2,8,256]{4,3,2,1,0:T(8,128)} fusion(bf16[16,10,2,8,256]{4,3,2,1,0:T(8,128)(2,1)S(1)} %bitcast.7), kind=kLoop, calls=%fused_computation | loop fusion | flops 1179648 | bytes 3538944 | tf_op jit(solution)/shard_map/div | solution.py:394

commit v3 on v2

--- a/solution.py
+++ b/solution.py
@@ -19,6 +19,7 @@
 QUARTER = NB // 2
 BLOCK = 128
 CHUNKS = QUARTER // BLOCK
+PIECES = 4
 MESH = pl.DeviceIdType.MESH
 F32 = jnp.float32
 BF16 = jnp.bfloat16
@@ -128,7 +129,7 @@
 
 
 def kernel(
-    n, pairs, x_ref, first_ref, second_ref, owner_col_ref, owner_row_ref, fwd_hbm, inv_hbm, out_ref,
+    n, pairs, x_ref, first_ref, second_ref, owner_ref, fwd_hbm, inv_hbm, out_ref,
     fwd_v, inv_v, xm, spec, white, a_v, b_v, cross, lagged, outgoing,
     fwd_sem, inv_sem, near_send, near_recv, far_send, far_recv, own_sem,
 ):
@@ -194,7 +195,10 @@
     level = jnp.sum(total, axis=1, keepdims=True) * (1.0 / NB)
     real_part, imag_part = spec[0], spec[1]
     scale = 1.0 / jnp.sqrt(real_part * real_part + imag_part * imag_part + 0.1 * level + 1e-06)
-    white[0, 0] = jnp.concatenate([real_part * scale, imag_part * scale], axis=0).astype(BF16)
+    result = jnp.concatenate([real_part * scale, imag_part * scale], axis=0).astype(BF16)
+    piece = NB // PIECES
+    for p in range(PIECES):
+        white[0, 0, p] = result[:, p * piece:(p + 1) * piece]
 
     pl.semaphore_wait(barrier, n)
     even = lax.rem(me, 2) == 0
@@ -204,93 +208,130 @@
     ahead = (lax.rem(me + 1, n), hour)
     across = (me, other)
 
-    def near_copy(src, dst, send, recv, device):
+    def near_copy(p, src, dst, kind, device):
         return pltpu.make_async_remote_copy(
-            src_ref=white.at[src[0], src[1]], dst_ref=white.at[dst[0], dst[1]],
-            send_sem=near_send.at[send], recv_sem=near_recv.at[recv], device_id=device, device_id_type=MESH,
+            src_ref=white.at[src[0], src[1], p], dst_ref=white.at[dst[0], dst[1], p],
+            send_sem=near_send.at[kind, p], recv_sem=near_recv.at[kind, p], device_id=device, device_id_type=MESH,
         )
 
-    copy_far = near_copy((0, 0), (0, 2), 0, 0, behind2)
-    copy_hour = near_copy((0, 0), (1, 0), 1, 1, across)
-    copy_both = near_copy((0, 2), (1, 2), 2, 2, across)
-    odd_own = near_copy((0, 0), (0, 1), 3, 3, behind)
-    even_own = near_copy((0, 2), (0, 1), 3, 3, ahead)
-    odd_other = near_copy((1, 0), (1, 1), 4, 4, behind)
-    even_other = near_copy((1, 2), (1, 1), 4, 4, ahead)
-
-    copy_far.start()
-    copy_hour.start()
+    def copy_far(p):
+        return near_copy(p, (0, 0), (0, 2), 0, behind2)
+
+    def copy_hour(p):
+        return near_copy(p, (0, 0), (1, 0), 1, across)
+
+    def copy_both(p):
+        return near_copy(p, (0, 2), (1, 2), 2, across) if p % 2 == 0 else near_copy(p, (1, 0), (1, 2), 2, behind2)
+
+    def odd_own(p):
+        return near_copy(p, (0, 0), (0, 1), 3, behind)
+
+    def even_own(p):
+        return near_copy(p, (0, 2), (0, 1), 3, ahead)
+
+    def odd_other(p):
+        return near_copy(p, (1, 0), (1, 1), 4, behind)
+
+    def even_other(p):
+        return near_copy(p, (1, 2), (1, 1), 4, ahead)
+
+    for p in range(PIECES):
+        copy_far(p).start()
+        copy_hour(p).start()
 
     @pl.when(odd)
     def _():
-        odd_own.start()
-
-    copy_far.wait_recv()
-    copy_both.start()
-
-    @pl.when(even)
-    def _():
-        even_own.start()
-
-    copy_hour.wait_recv()
-
-    @pl.when(odd)
-    def _():
-        odd_other.start()
-
-    half_rows = rows
+        for p in range(PIECES):
+            odd_own(p).start()
+
     group = 2 * rows
     wide = lax.broadcasted_iota(jnp.int32, (pairs, 3 * group), 1)
-    first, second = first_ref[...], second_ref[...]
-    second_base = second // 8 * group + second % 8 * COMPS
+    row_of = lax.broadcasted_iota(jnp.int32, (pairs, pairs), 0)
+    column_of = lax.broadcasted_iota(jnp.int32, (pairs, pairs), 1)
+
+    def upright(ref):
+        return jnp.sum(jnp.where(row_of == column_of, ref[...], 0), axis=1, keepdims=True)
+
+    first, second = upright(first_ref), upright(second_ref)
+    second_base = second // 8 * group + second % 8
     pick_a, pick_b = [], []
     for part in range(2):
+        for comp in range(2):
+            shift = part * rows + (comp + hour) * 8
+            pick_a.append(jnp.where(wide[:, :group] == first + shift, 1.0, 0.0))
         for comp in range(COMPS):
-            shift = part * half_rows + comp
-            pick_a.append(jnp.where(wide[:, :group] == first * COMPS + shift, 1.0, 0.0))
-            pick_b.append(jnp.where(wide == second_base + shift, 1.0, 0.0))
+            pick_b.append(jnp.where(wide == second_base + (part * rows + comp * 8), 1.0, 0.0))
     pick_a = jnp.concatenate(pick_a, axis=0).astype(BF16)
     pick_b = jnp.concatenate(pick_b, axis=0).astype(BF16)
-    order_col = lax.broadcasted_iota(jnp.int32, (pairs, 2 * pairs), 0)
-    order_row = lax.broadcasted_iota(jnp.int32, (pairs, 2 * pairs), 1) % pairs
-    owner_row = owner_row_ref[...]
-    earlier = (owner_col_ref[...] == owner_row) & (order_col < order_row)
-    slot = jnp.sum(jnp.where(earlier, 1, 0), axis=0, keepdims=True)
+    owner_row = owner_ref[...]
+    earlier = (upright(owner_ref) == owner_row) & (row_of < column_of)
+    place_of = owner_row * 16 + jnp.sum(jnp.where(earlier, 1, 0), axis=0, keepdims=True)
+    twice = lax.broadcasted_iota(jnp.int32, (pairs, 2 * pairs), 1) % pairs
+    twice = jnp.where(twice == lax.broadcasted_iota(jnp.int32, (pairs, 2 * pairs), 0), 1.0, 0.0).astype(BF16)
+    place_of = jnp.broadcast_to(place_of, (8, pairs)).astype(F32).astype(BF16)
+    place_of = jnp.dot(place_of, twice, preferred_element_type=F32)[0:1]
     side = lax.broadcasted_iota(jnp.int32, (1, 2 * pairs), 1) // pairs
-    target = owner_row * 16 + side * 8 + slot
-    place = jnp.where(lax.broadcasted_iota(jnp.int32, (16 * n, 2 * pairs), 0) == target, 1.0, 0.0).astype(BF16)
-
-    copy_both.wait_recv()
-
-    @pl.when(even)
-    def _():
-        even_other.start()
-
-    odd_own.wait_recv()
-    odd_other.wait_recv()
+    target = place_of + (side * 8).astype(F32)
+    spot = lax.broadcasted_iota(jnp.int32, (16 * n, 2 * pairs), 0).astype(F32)
+    place = jnp.where(spot == target, 1.0, 0.0).astype(BF16)
+
+    for p in range(PIECES):
+        copy_far(p).wait_recv()
+        if p % 2 == 0:
+            copy_both(p).start()
+
+        @pl.when(even)
+        def _(p=p):
+            even_own(p).start()
+
+        copy_hour(p).wait_recv()
+        if p % 2 == 1:
+            copy_both(p).start()
+
+        @pl.when(odd)
+        def _(p=p):
+            odd_other(p).start()
 
     step = 256
 
-    def correlate(q, carry):
-        lanes = pl.ds(pl.multiple_of(q * step, step), step)
-        for h in range(2):
-            a_v[h] = jnp.dot(pick_a, white[h, 0, :, lanes], preferred_element_type=F32).reshape(2, COMPS, pairs, step)
-            b_v[h] = jnp.dot(
-                pick_b, white[h, :, :, lanes].reshape(3 * group, step), preferred_element_type=F32
-            ).reshape(2, COMPS, pairs, step)
-        for i in range(5):
-            kind = hour * 4 + i
-            c, e = kind // COMPS, kind % COMPS
-            re, im = 0.0, 0.0
+    def correlate(p):
+        def body(q, carry):
+            lanes = pl.ds(pl.multiple_of(q * step, step), step)
             for h in range(2):
-                ar, ai, br, bi = a_v[h, 0, c], a_v[h, 1, c], b_v[h, 0, e], b_v[h, 1, e]
-                re = re + (ar * br + ai * bi)
-                im = im + (ar * bi - ai * br)
-            cross[pl.ds(i * pairs, pairs), lanes] = re.astype(BF16)
-            cross[pl.ds(i * pairs, pairs), pl.ds(pl.multiple_of(NB + q * step, step), step)] = im.astype(BF16)
-        return carry
-
-    lax.fori_loop(0, NB // step, correlate, 0)
+                a_v[h] = jnp.dot(pick_a, white[h, 0, p, :, lanes], preferred_element_type=F32).reshape(2, 2, pairs, step)
+                b_v[h] = jnp.dot(
+                    pick_b, white[h, :, p, :, lanes].reshape(3 * group, step), preferred_element_type=F32
+                ).reshape(2, COMPS, pairs, step)
+            start = p * piece + q * step
+            for i in range(5):
+                kind = hour * 4 + i
+                c, e = kind // COMPS - hour, kind % COMPS
+                re, im = 0.0, 0.0
+                for h in range(2):
+                    ar, ai, br, bi = a_v[h, 0, c], a_v[h, 1, c], b_v[h, 0, e], b_v[h, 1, e]
+                    re = re + (ar * br + ai * bi)
+                    im = im + (ar * bi - ai * br)
+                cross[pl.ds(i * pairs, pairs), pl.ds(pl.multiple_of(start, step), step)] = re.astype(BF16)
+                cross[pl.ds(i * pairs, pairs), pl.ds(pl.multiple_of(NB + start, step), step)] = im.astype(BF16)
+            return carry
+
+        lax.fori_loop(0, piece // step, body, 0)
+
+    def pass_on(p):
+        copy_both(p).wait_recv()
+
+        @pl.when(even)
+        def _():
+            even_other(p).start()
+
+    pass_on(0)
+    for p in range(PIECES):
+        if p + 1 < PIECES:
+            pass_on(p + 1)
+        odd_own(p).wait_recv()
+        odd_other(p).wait_recv()
+        correlate(p)
+
     for c in range(4):
         inv_copy(c).wait()
 
@@ -322,11 +363,18 @@
             moved = jnp.dot(place, both, preferred_element_type=F32).astype(BF16)
             outgoing[:, i, part] = moved.reshape(n, 16, 256)
 
+        home = me // 8 * 8
+
         def send(step, carry, part=part):
-            far_copy(part, me, lax.rem(me + step, n)).start()
+            far_copy(part, me, lax.rem(home + 8, n) + lax.rem(me + step, 8)).start()
+
+            @pl.when(step > 0)
+            def _():
+                far_copy(part, me, home + lax.rem(me + step, 8)).start()
+
             return carry
 
-        lax.fori_loop(1, n, send, 0)
+        lax.fori_loop(0, 8, send, 0)
         own_copy(part).start()
 
     def finish(step, carry):
@@ -340,11 +388,9 @@
     lax.fori_loop(1, n, finish, 0)
     for part in range(2):
         own_copy(part).wait()
-    copy_far.wait_send()
-    copy_hour.wait_send()
-    copy_both.wait_send()
-    odd_own.wait_send()
-    odd_other.wait_send()
+    for p in range(PIECES):
+        for copy in (copy_far(p), copy_hour(p), copy_both(p), odd_own(p), odd_other(p)):
+            copy.wait_send()
 
 
 def shards(windows, pair_first, pair_second, owners):
@@ -357,23 +403,23 @@
     received = pl.pallas_call(
         functools.partial(kernel, n, pairs),
         out_shape=jax.ShapeDtypeStruct((n, 5, 2, 16, 256), BF16),
-        in_specs=[vmem] * 5 + [anywhere] * 2,
+        in_specs=[vmem] * 4 + [anywhere] * 2,
         out_specs=anywhere,
         scratch_shapes=[
             pltpu.VMEM(fwd.shape, BF16),
             pltpu.VMEM(inv.shape, BF16),
             pltpu.VMEM((8 * rows, HALF), BF16),
             pltpu.VMEM((2, rows, NB), F32),
-            pltpu.VMEM((2, 3, 2 * rows, NB), BF16),
-            pltpu.VMEM((2, 2, COMPS, pairs, 256), F32),
+            pltpu.VMEM((2, 3, PIECES, 2 * rows, NB // PIECES), BF16),
+            pltpu.VMEM((2, 2, 2, pairs, 256), F32),
             pltpu.VMEM((2, 2, COMPS, pairs, 256), F32),
             pltpu.VMEM((5 * pairs, 2 * NB), BF16),
             pltpu.VMEM((2, 5 * pairs, 256), BF16),
             pltpu.VMEM((n, 5, 2, 16, 256), BF16),
             pltpu.SemaphoreType.DMA((CHUNKS,)),
             pltpu.SemaphoreType.DMA((4,)),
-            pltpu.SemaphoreType.DMA((5,)),
-            pltpu.SemaphoreType.DMA((5,)),
+            pltpu.SemaphoreType.DMA((5, PIECES)),
+            pltpu.SemaphoreType.DMA((5, PIECES)),
             pltpu.SemaphoreType.DMA((2, n)),
             pltpu.SemaphoreType.DMA((2, n)),
             pltpu.SemaphoreType.DMA((2,)),
@@ -382,11 +428,10 @@
             collective_id=0, has_side_effects=True, vmem_limit_bytes=50 * 2**20
         ),
     )(
-        windows.reshape(rows, SAMPLES),
-        pair_first[:, None],
-        pair_second[:, None],
-        owners,
-        jnp.tile(owners[:, 0], 2)[None, :],
+        windows[0].transpose(1, 0, 2).reshape(rows, SAMPLES),
+        pair_first[None, :],
+        pair_second[None, :],
+        owners.reshape(1, pairs),
         fwd,
         inv,
     )

time: 60.6 us -> 58.2 us (0.960)
  the two profiles are of different devices: /device:TPU:11 before, /device:TPU:0 now
where the time goes in v3:
time: 58.2 us; the launch traced here: 58 us
  Pallas kernels  53.4 us (92%)
  local copies, waits for them, and re-layouts  2.89 us (5%)
  other arithmetic  1.71 us (3%)
    pallas_call x1, Pallas kernels, shards(): pl.pallas_call(functools.partial(kernel, n, pairs), out_shape=jax.ShapeDt...  53.4 us
    unnamed x8, local copies, waits for them, and re-layouts  2.89 us
    div x1, other arithmetic, shards(): return received.astype(F32) / jnp.sqrt(F32(2 * NB))  1.71 us

profile of v3, /device:TPU:0, one launch (start us, length us, event | category | flops | bytes accessed | tf_op | source)
XLA Modules:
  0.0 58.0 jit_solution(13368863376052514665)
XLA Ops:
  0.0 0.0 copy-start
  0.0 0.9 %copy-done = bf16[1,8,3,4096]{3,1,2,0:T(8,128)(2,1)S(1)} copy-done((bf16[1,8,3,4096]{3,1,2,0:T(8,128)(2,1)S(1)}, bf16[1,8,3,4096]{3,1,2,0:T(8,128)(2,1)}, u32[]{:S(2)}) %copy-start) | copy-done | bytes 196632
  0.9 0.0 copy-start.1
  0.9 0.7 %copy-done.1 = s32[64]{0:T(128)S(1)} copy-done((s32[64]{0:T(128)S(1)}, s32[64]{0:T(128)}, u32[]{:S(2)}) %copy-start.1) | copy-done | bytes 280
  1.6 0.0 copy-start.2
  1.6 0.7 %copy-done.2 = s32[64]{0:T(128)S(1)} copy-done((s32[64]{0:T(128)S(1)}, s32[64]{0:T(128)}, u32[]{:S(2)}) %copy-start.2) | copy-done | bytes 280
  2.2 0.0 copy-start.3
  2.2 0.7 %copy-done.3 = s32[64,1]{0,1:T(1,128)S(1)} copy-done((s32[64,1]{0,1:T(1,128)S(1)}, s32[64,1]{0,1:T(1,128)}, u32[]{:S(2)}) %copy-start.3) | copy-done | bytes 280
  2.9 53.4 %shard_map.64 = bf16[16,5,2,16,256]{4,3,2,1,0:T(8,128)(2,1)S(1)} custom-call(bf16[24,4096]{1,0:T(8,128)(2,1)S(1)} %bitcast.13, s32[1,64]{1,0:T(1,128)S(1)} %bitcast.14, s32[1,64]{1,0:T(1,128)S(1)} %bitcast.15, s32[1,64]{1,0:T(1,128)S(1)} %bitcast.16, bf16[8,2048,256]{2,1,0:T(8,128)(2,1)} %constant.7.clone.fwd_hbm, bf16[4,4096,256]{2,1,0:T(8,128)(2,1)} %constant.8.clone.inv_hbm), custom_call_target="tpu_custom_call" | custom-call | tf_op jit(solution)/shard_map/pallas_call | solution.py:403
  56.3 1.7 %convert_multiply_fusion = f32[16,9,2,8,256]{4,3,2,1,0:T(8,128)} fusion(bf16[16,10,2,8,256]{4,3,2,1,0:T(8,128)(2,1)S(1)} %bitcast.12), kind=kLoop, calls=%fused_computation | loop fusion | flops 1179648 | bytes 3538944 | tf_op jit(solution)/shard_map/div | solution.py:439
Async XLA Ops:
  0.0 0.9 %copy-start = (bf16[1,8,3,4096]{3,1,2,0:T(8,128)(2,1)S(1)}, bf16[1,8,3,4096]{3,1,2,0:T(8,128)(2,1)}, u32[]{:S(2)}) copy-start(bf16[1,8,3,4096]{3,1,2,0:T(8,128)(2,1)} %param.6) | copy-start | bytes 589828
  0.9 0.7 %copy-start.1 = (s32[64]{0:T(128)S(1)}, s32[64]{0:T(128)}, u32[]{:S(2)}) copy-start(s32[64]{0:T(128)} %param.7) | copy-start | bytes 772
  1.6 0.7 %copy-start.2 = (s32[64]{0:T(128)S(1)}, s32[64]{0:T(128)}, u32[]{:S(2)}) copy-start(s32[64]{0:T(128)} %param.8) | copy-start | bytes 772
  2.2 0.7 %copy-start.3 = (s32[64,1]{0,1:T(1,128)S(1)}, s32[64,1]{0,1:T(1,128)}, u32[]{:S(2)}) copy-start(s32[64,1]{0,1:T(1,128)} %param.9) | copy-start | bytes 772

commit v4 on v3

--- a/solution.py
+++ b/solution.py
@@ -129,22 +129,20 @@
 
 
 def kernel(
-    n, pairs, x_ref, first_ref, second_ref, owner_ref, fwd_hbm, inv_hbm, out_ref,
-    fwd_v, inv_v, xm, spec, white, a_v, b_v, cross, lagged, outgoing,
+    n, pairs, x_hbm, first_hbm, second_hbm, owner_hbm, fwd_hbm, inv_hbm, out_ref,
+    x_ref, first_ref, second_ref, owner_ref, in_sem, fwd_v, inv_v, xm, spec, white, a_v, b_v, early, cross, lagged, outgoing,
     fwd_sem, inv_sem, near_send, near_recv, far_send, far_recv, own_sem,
 ):
     me = lax.axis_index("sens")
     hour = lax.axis_index("hour")
     other = 1 - hour
 
-    barrier = pltpu.get_barrier_semaphore()
-
-    def greet(step, carry):
-        pl.semaphore_signal(barrier, inc=1, device_id=(lax.rem(me + step, n), hour), device_id_type=MESH)
-        return carry
-
-    lax.fori_loop(1, n, greet, 0)
-    pl.semaphore_signal(barrier, inc=1, device_id=(me, other), device_id_type=MESH)
+    inputs = [
+        pltpu.make_async_copy(source, target, in_sem.at[k])
+        for k, (source, target) in enumerate(
+            ((x_hbm, x_ref), (first_hbm, first_ref), (second_hbm, second_ref), (owner_hbm, owner_ref))
+        )
+    ]
 
     def fwd_copy(c):
         return pltpu.make_async_copy(fwd_hbm.at[c], fwd_v.at[c], fwd_sem.at[c])
@@ -152,10 +150,24 @@
     def inv_copy(c):
         return pltpu.make_async_copy(inv_hbm.at[c], inv_v.at[c], inv_sem.at[c])
 
+    for copy in inputs:
+        copy.start()
     for c in range(CHUNKS):
         fwd_copy(c).start()
     for c in range(4):
         inv_copy(c).start()
+
+    barrier = pltpu.get_barrier_semaphore()
+
+    def greet(step, carry):
+        pl.semaphore_signal(barrier, inc=1, device_id=(lax.rem(me + step, n), hour), device_id_type=MESH)
+        return carry
+
+    lax.fori_loop(1, n, greet, 0)
+    pl.semaphore_signal(barrier, inc=1, device_id=(me, other), device_id_type=MESH)
+
+    for copy in inputs:
+        copy.wait()
 
     rows = x_ref.shape[0]
     x = x_ref[...].astype(F32)
@@ -275,13 +287,15 @@
     spot = lax.broadcasted_iota(jnp.int32, (16 * n, 2 * pairs), 0).astype(F32)
     place = jnp.where(spot == target, 1.0, 0.0).astype(BF16)
 
-    for p in range(PIECES):
+    step = 256
+
+    def arrive(p):
         copy_far(p).wait_recv()
         if p % 2 == 0:
             copy_both(p).start()
 
         @pl.when(even)
-        def _(p=p):
+        def _():
             even_own(p).start()
 
         copy_hour(p).wait_recv()
@@ -289,48 +303,61 @@
             copy_both(p).start()
 
         @pl.when(odd)
-        def _(p=p):
+        def _():
             odd_other(p).start()
 
-    step = 256
-
-    def correlate(p):
+    def pass_on(p):
+        copy_both(p).wait_recv()
+
+        @pl.when(even)
+        def _():
+            even_other(p).start()
+
+    def correlate(p, h):
+        (odd_own, odd_other)[h](p).wait_recv()
+
         def body(q, carry):
             lanes = pl.ds(pl.multiple_of(q * step, step), step)
-            for h in range(2):
-                a_v[h] = jnp.dot(pick_a, white[h, 0, p, :, lanes], preferred_element_type=F32).reshape(2, 2, pairs, step)
-                b_v[h] = jnp.dot(
-                    pick_b, white[h, :, p, :, lanes].reshape(3 * group, step), preferred_element_type=F32
-                ).reshape(2, COMPS, pairs, step)
+            a_v[...] = jnp.dot(pick_a, white[h, 0, p, :, lanes], preferred_element_type=F32).reshape(2, 2, pairs, step)
+            b_v[...] = jnp.dot(
+                pick_b, white[h, :, p, :, lanes].reshape(3 * group, step), preferred_element_type=F32
+            ).reshape(2, COMPS, pairs, step)
             start = p * piece + q * step
+            real_lanes = pl.ds(pl.multiple_of(start, step), step)
+            imag_lanes = pl.ds(pl.multiple_of(NB + start, step), step)
             for i in range(5):
                 kind = hour * 4 + i
                 c, e = kind // COMPS - hour, kind % COMPS
-                re, im = 0.0, 0.0
-                for h in range(2):
-                    ar, ai, br, bi = a_v[h, 0, c], a_v[h, 1, c], b_v[h, 0, e], b_v[h, 1, e]
-                    re = re + (ar * br + ai * bi)
-                    im = im + (ar * bi - ai * br)
-                cross[pl.ds(i * pairs, pairs), pl.ds(pl.multiple_of(start, step), step)] = re.astype(BF16)
-                cross[pl.ds(i * pairs, pairs), pl.ds(pl.multiple_of(NB + start, step), step)] = im.astype(BF16)
+                ar, ai, br, bi = a_v[0, c], a_v[1, c], b_v[0, e], b_v[1, e]
+                re = ar * br + ai * bi
+                im = ar * bi - ai * br
+                here = pl.ds(i * pairs, pairs)
+                if h == 0:
+                    early[here, real_lanes] = re
+                    early[here, imag_lanes] = im
+                else:
+                    cross[here, real_lanes] = (early[here, real_lanes] + re).astype(BF16)
+                    cross[here, imag_lanes] = (early[here, imag_lanes] + im).astype(BF16)
             return carry
 
         lax.fori_loop(0, piece // step, body, 0)
 
-    def pass_on(p):
-        copy_both(p).wait_recv()
-
-        @pl.when(even)
-        def _():
-            even_other(p).start()
-
+    arrive(0)
+    arrive(1)
+    correlate(0, 0)
+    arrive(2)
+    correlate(1, 0)
+    arrive(3)
+    correlate(2, 0)
     pass_on(0)
-    for p in range(PIECES):
-        if p + 1 < PIECES:
-            pass_on(p + 1)
-        odd_own(p).wait_recv()
-        odd_other(p).wait_recv()
-        correlate(p)
+    correlate(3, 0)
+    pass_on(1)
+    correlate(0, 1)
+    pass_on(2)
+    correlate(1, 1)
+    pass_on(3)
+    correlate(2, 1)
+    correlate(3, 1)
 
     for c in range(4):
         inv_copy(c).wait()
@@ -398,21 +425,26 @@
     rows = windows.shape[1] * COMPS
     pairs = pair_first.shape[0]
     fwd, inv = (jnp.asarray(table) for table in folded_tables())
-    vmem = pl.BlockSpec(memory_space=pltpu.VMEM)
     anywhere = pl.BlockSpec(memory_space=pl.ANY)
     received = pl.pallas_call(
         functools.partial(kernel, n, pairs),
         out_shape=jax.ShapeDtypeStruct((n, 5, 2, 16, 256), BF16),
-        in_specs=[vmem] * 4 + [anywhere] * 2,
+        in_specs=[pl.BlockSpec(memory_space=pltpu.HBM)] * 6,
         out_specs=anywhere,
         scratch_shapes=[
+            pltpu.VMEM((rows, SAMPLES), BF16),
+            pltpu.VMEM((1, pairs), jnp.int32),
+            pltpu.VMEM((1, pairs), jnp.int32),
+            pltpu.VMEM((1, pairs), jnp.int32),
+            pltpu.SemaphoreType.DMA((4,)),
             pltpu.VMEM(fwd.shape, BF16),
             pltpu.VMEM(inv.shape, BF16),
             pltpu.VMEM((8 * rows, HALF), BF16),
             pltpu.VMEM((2, rows, NB), F32),
             pltpu.VMEM((2, 3, PIECES, 2 * rows, NB // PIECES), BF16),
-            pltpu.VMEM((2, 2, 2, pairs, 256), F32),
-            pltpu.VMEM((2, 2, COMPS, pairs, 256), F32),
+            pltpu.VMEM((2, 2, pairs, 256), F32),
+            pltpu.VMEM((2, COMPS, pairs, 256), F32),
+            pltpu.VMEM((5 * pairs, 2 * NB), F32),
             pltpu.VMEM((5 * pairs, 2 * NB), BF16),
             pltpu.VMEM((2, 5 * pairs, 256), BF16),
             pltpu.VMEM((n, 5, 2, 16, 256), BF16),
@@ -425,7 +457,7 @@
             pltpu.SemaphoreType.DMA((2,)),
         ],
         compiler_params=pltpu.CompilerParams(
-            collective_id=0, has_side_effects=True, vmem_limit_bytes=50 * 2**20
+            collective_id=0, has_side_effects=True, vmem_limit_bytes=56 * 2**20
         ),
     )(
         windows[0].transpose(1, 0, 2).reshape(rows, SAMPLES),

time: 58.2 us -> 57.6 us (0.990)
  local copies, waits for them, and re-layouts: 2.89 us -> 0 us
  other arithmetic: 1.71 us -> 3.01 us
  Pallas kernels: 53.4 us -> 54.4 us
    unnamed x8 -> x0, local copies, waits for them, and re-layouts: 2.89 us -> none
    div x1, other arithmetic: 1.71 us -> 3.01 us  [shards(): return received.astype(F32) / jnp.sqrt(F32(2 * NB))]
    pallas_call x1, Pallas kernels: 53.4 us -> 54.4 us  [shards(): pl.pallas_call(functools.partial(kernel, n, pairs), out_shape=jax.ShapeDt...]
where the time goes in v4:
time: 57.6 us; the launch traced here: 57.4 us
  Pallas kernels  54.4 us (94%)
  other arithmetic  3.01 us (5%)
    pallas_call x1, Pallas kernels, shards(): pl.pallas_call(functools.partial(kernel, n, pairs), out_shape=jax.ShapeDt...  54.4 us
    div x1, other arithmetic, shards(): return received.astype(F32) / jnp.sqrt(F32(2 * NB))  3.01 us

profile of v4, /device:TPU:0, one launch (start us, length us, event | category | flops | bytes accessed | tf_op | source)
XLA Modules:
  0.0 57.4 jit_solution(12617903579359926583)
XLA Ops:
  0.0 54.4 %shard_map.64 = bf16[16,5,2,16,256]{4,3,2,1,0:T(8,128)(2,1)} custom-call(bf16[24,4096]{1,0:T(8,128)(2,1)} %bitcast.13, s32[1,64]{1,0:T(1,128)} %bitcast.14, s32[1,64]{1,0:T(1,128)} %bitcast.15, s32[1,64]{1,0:T(1,128)} %bitcast.16, bf16[8,2048,256]{2,1,0:T(8,128)(2,1)} %constant.7.clone.fwd_hbm, bf16[4,4096,256]{2,1,0:T(8,128)(2,1)} %constant.8.clone.inv_hbm), custom_call_target="tpu_custom_call" | custom-call | tf_op jit(solution)/shard_map/pallas_call | solution.py:429
  54.4 3.0 %convert_multiply_fusion = f32[16,9,2,8,256]{4,3,2,1,0:T(8,128)} fusion(bf16[16,10,2,8,256]{4,3,2,1,0:T(8,128)(2,1)} %bitcast.12), kind=kLoop, calls=%fused_computation | loop fusion | flops 1179648 | bytes 3538944 | tf_op jit(solution)/shard_map/div | solution.py:471

commit v5 on v4

--- a/solution.py
+++ b/solution.py
@@ -154,8 +154,6 @@
         copy.start()
     for c in range(CHUNKS):
         fwd_copy(c).start()
-    for c in range(4):
-        inv_copy(c).start()
 
     barrier = pltpu.get_barrier_semaphore()
 
@@ -204,6 +202,8 @@
         return total + (re_a * re_a + im_a * im_a) + (re_b * re_b + im_b * im_b)
 
     total = lax.fori_loop(0, CHUNKS, transform, jnp.zeros((rows, BLOCK), F32))
+    for c in range(4):
+        inv_copy(c).start()
     level = jnp.sum(total, axis=1, keepdims=True) * (1.0 / NB)
     real_part, imag_part = spec[0], spec[1]
     scale = 1.0 / jnp.sqrt(real_part * real_part + imag_part * imag_part + 0.1 * level + 1e-06)
@@ -362,33 +362,31 @@
     for c in range(4):
         inv_copy(c).wait()
 
+    spans = (pl.ds(0, 5), pl.ds(5, 4))
+
     def far_copy(part, source, dst):
-        count = 5 - part
         return pltpu.make_async_remote_copy(
-            src_ref=outgoing.at[dst, pl.ds(0, count), part], dst_ref=out_ref.at[source, pl.ds(0, count), part],
+            src_ref=outgoing.at[dst, spans[part]], dst_ref=out_ref.at[source, spans[part]],
             send_sem=far_send.at[part, dst], recv_sem=far_recv.at[part, source],
             device_id=(dst, hour), device_id_type=MESH,
         )
 
     def own_copy(part):
-        count = 5 - part
-        return pltpu.make_async_copy(
-            outgoing.at[me, pl.ds(0, count), part], out_ref.at[me, pl.ds(0, count), part], own_sem.at[part]
-        )
+        return pltpu.make_async_copy(outgoing.at[me, spans[part]], out_ref.at[me, spans[part]], own_sem.at[part])
 
     for part in range(2):
-        count = 5 - part
-        first_row = pl.multiple_of(part * hour * pairs, pairs)
-        lag_half = hour if part == 0 else other
-        source = cross[pl.ds(first_row, count * pairs), :]
-        for side in range(2):
-            lagged[side, pl.ds(0, count * pairs)] = jnp.dot(
-                source, inv_v[lag_half * 2 + side], preferred_element_type=F32
-            ).astype(BF16)
-        for i in range(count):
-            both = lagged[:, pl.ds(i * pairs, pairs)].reshape(2 * pairs, 256)
-            moved = jnp.dot(place, both, preferred_element_type=F32).astype(BF16)
-            outgoing[:, i, part] = moved.reshape(n, 16, 256)
+        for lag_half, units, skip in ((hour, ((0, 2, 4), (6, 8))[part], 0), (other, ((1, 3), (5, 7))[part], hour)):
+            count = len(units)
+            first_row = pl.multiple_of((units[0] // 2 + skip) * pairs, pairs)
+            source = cross[pl.ds(first_row, count * pairs), :]
+            for side in range(2):
+                lagged[side, pl.ds(0, count * pairs)] = jnp.dot(
+                    source, inv_v[lag_half * 2 + side], preferred_element_type=F32
+                ).astype(BF16)
+            for i, unit in enumerate(units):
+                both = lagged[:, pl.ds(i * pairs, pairs)].reshape(2 * pairs, 256)
+                moved = jnp.dot(place, both, preferred_element_type=F32).astype(BF16)
+                outgoing[:, unit] = moved.reshape(n, 16, 256)
 
         home = me // 8 * 8
 
@@ -425,12 +423,11 @@
     rows = windows.shape[1] * COMPS
     pairs = pair_first.shape[0]
     fwd, inv = (jnp.asarray(table) for table in folded_tables())
-    anywhere = pl.BlockSpec(memory_space=pl.ANY)
     received = pl.pallas_call(
         functools.partial(kernel, n, pairs),
-        out_shape=jax.ShapeDtypeStruct((n, 5, 2, 16, 256), BF16),
+        out_shape=jax.ShapeDtypeStruct((n, 9, 16, 256), BF16),
         in_specs=[pl.BlockSpec(memory_space=pltpu.HBM)] * 6,
-        out_specs=anywhere,
+        out_specs=pl.BlockSpec(memory_space=pltpu.VMEM),
         scratch_shapes=[
             pltpu.VMEM((rows, SAMPLES), BF16),
             pltpu.VMEM((1, pairs), jnp.int32),
@@ -446,8 +443,8 @@
             pltpu.VMEM((2, COMPS, pairs, 256), F32),
             pltpu.VMEM((5 * pairs, 2 * NB), F32),
             pltpu.VMEM((5 * pairs, 2 * NB), BF16),
-            pltpu.VMEM((2, 5 * pairs, 256), BF16),
-            pltpu.VMEM((n, 5, 2, 16, 256), BF16),
+            pltpu.VMEM((2, 3 * pairs, 256), BF16),
+            pltpu.VMEM((n, 9, 16, 256), BF16),
             pltpu.SemaphoreType.DMA((CHUNKS,)),
             pltpu.SemaphoreType.DMA((4,)),
             pltpu.SemaphoreType.DMA((5, PIECES)),
@@ -457,7 +454,7 @@
             pltpu.SemaphoreType.DMA((2,)),
         ],
         compiler_params=pltpu.CompilerParams(
-            collective_id=0, has_side_effects=True, vmem_limit_bytes=56 * 2**20
+            collective_id=0, has_side_effects=True, vmem_limit_bytes=44 * 2**20
         ),
     )(
         windows[0].transpose(1, 0, 2).reshape(rows, SAMPLES),
@@ -467,7 +464,7 @@
         fwd,
         inv,
     )
-    received = received.reshape(n, 10, 2, 8, 256)[:, :9].transpose(0, 3, 1, 2, 4).reshape(n * 8, WIDTH // 2)
+    received = received.reshape(n, 9, 2, 8, 256).transpose(0, 3, 1, 2, 4).reshape(n * 8, WIDTH // 2)
     return received.astype(F32) / jnp.sqrt(F32(2 * NB))
 
 

time: 57.6 us -> 59 us (1.024)
  local copies, waits for them, and re-layouts: 0 us -> 6.27 us
  Pallas kernels: 54.4 us -> 50.8 us
  other arithmetic: 3.01 us -> 1.74 us
    unnamed x0 -> x10, local copies, waits for them, and re-layouts: none -> 6.27 us
    pallas_call x1, Pallas kernels: 54.4 us -> 50.8 us  [shards(): pl.pallas_call(functools.partial(kernel, n, pairs), out_shape=jax.ShapeDt...]
    div x1, other arithmetic: 3.01 us -> 1.74 us  [shards(): return received.astype(F32) / jnp.sqrt(F32(2 * NB))]
where the time goes in v5:
time: 59 us; the launch traced here: 58.8 us
  Pallas kernels  50.8 us (86%)
  local copies, waits for them, and re-layouts  6.27 us (11%)
  other arithmetic  1.74 us (3%)
    pallas_call x1, Pallas kernels, shards(): pl.pallas_call(functools.partial(kernel, n, pairs), out_shape=jax.ShapeDt...  50.8 us
    unnamed x10, local copies, waits for them, and re-layouts  6.27 us
    div x1, other arithmetic, shards(): return received.astype(F32) / jnp.sqrt(F32(2 * NB))  1.74 us

profile of v5, /device:TPU:0, one launch (start us, length us, event | category | flops | bytes accessed | tf_op | source)
XLA Modules:
  0.0 58.8 jit_solution(9327400017790351463)
XLA Ops:
  0.0 0.0 copy-start
  0.0 3.4 %copy-done = bf16[8,2048,256]{2,1,0:T(8,128)(2,1)S(1)} copy-done((bf16[8,2048,256]{2,1,0:T(8,128)(2,1)S(1)}, bf16[8,2048,256]{2,1,0:T(8,128)(2,1)}, u32[]{:S(2)}) %copy-start) | copy-done | bytes 8388632
  3.4 0.0 copy-start.1
  3.4 0.9 %copy-done.1 = bf16[1,8,3,4096]{3,1,2,0:T(8,128)(2,1)S(1)} copy-done((bf16[1,8,3,4096]{3,1,2,0:T(8,128)(2,1)S(1)}, bf16[1,8,3,4096]{3,1,2,0:T(8,128)(2,1)}, u32[]{:S(2)}) %copy-start.1) | copy-done | bytes 196632
  4.3 0.0 copy-start.2
  4.3 0.7 %copy-done.2 = s32[64]{0:T(128)S(1)} copy-done((s32[64]{0:T(128)S(1)}, s32[64]{0:T(128)}, u32[]{:S(2)}) %copy-start.2) | copy-done | bytes 280
  5.0 0.0 copy-start.3
  5.0 0.7 %copy-done.3 = s32[64]{0:T(128)S(1)} copy-done((s32[64]{0:T(128)S(1)}, s32[64]{0:T(128)}, u32[]{:S(2)}) %copy-start.3) | copy-done | bytes 280
  5.6 0.0 copy-start.4
  5.6 0.7 %copy-done.4 = s32[64,1]{0,1:T(1,128)S(1)} copy-done((s32[64,1]{0,1:T(1,128)S(1)}, s32[64,1]{0,1:T(1,128)}, u32[]{:S(2)}) %copy-start.4) | copy-done | bytes 280
  6.3 50.8 %shard_map.64 = bf16[16,9,16,256]{3,2,1,0:T(8,128)(2,1)S(1)} custom-call(bf16[24,4096]{1,0:T(8,128)(2,1)S(1)} %bitcast.13, s32[1,64]{1,0:T(1,128)S(1)} %bitcast.14, s32[1,64]{1,0:T(1,128)S(1)} %bitcast.15, s32[1,64]{1,0:T(1,128)S(1)} %bitcast.16, bf16[8,2048,256]{2,1,0:T(8,128)(2,1)S(1)} %copy-done, bf16[4,4096,256]{2,1,0:T(8,128)(2,1)} %constant.8.clone.inv_hbm), custom_call_target="tpu_custom_call" | custom-call | tf_op jit(solution)/shard_map/pallas_call | solution.py:426
  57.1 1.7 %convert_multiply_fusion = f32[16,9,16,256]{3,2,1,0:T(8,128)} fusion(bf16[16,9,16,256]{3,2,1,0:T(8,128)(2,1)S(1)} %shard_map.64), kind=kLoop, calls=%fused_computation | loop fusion | flops 1179648 | bytes 3538944 | tf_op jit(solution)/shard_map/div | solution.py:468
Async XLA Ops:
  0.0 3.4 %copy-start = (bf16[8,2048,256]{2,1,0:T(8,128)(2,1)S(1)}, bf16[8,2048,256]{2,1,0:T(8,128)(2,1)}, u32[]{:S(2)}) copy-start(bf16[8,2048,256]{2,1,0:T(8,128)(2,1)} %constant.7.clone.fwd_hbm) | copy-start | bytes 25165828
  3.4 0.9 %copy-start.1 = (bf16[1,8,3,4096]{3,1,2,0:T(8,128)(2,1)S(1)}, bf16[1,8,3,4096]{3,1,2,0:T(8,128)(2,1)}, u32[]{:S(2)}) copy-start(bf16[1,8,3,4096]{3,1,2,0:T(8,128)(2,1)} %param.6) | copy-start | bytes 589828
  4.3 0.7 %copy-start.2 = (s32[64]{0:T(128)S(1)}, s32[64]{0:T(128)}, u32[]{:S(2)}) copy-start(s32[64]{0:T(128)} %param.7) | copy-start | bytes 772
  5.0 0.7 %copy-start.3 = (s32[64]{0:T(128)S(1)}, s32[64]{0:T(128)}, u32[]{:S(2)}) copy-start(s32[64]{0:T(128)} %param.8) | copy-start | bytes 772
  5.6 0.7 %copy-start.4 = (s32[64,1]{0,1:T(1,128)S(1)}, s32[64,1]{0,1:T(1,128)}, u32[]{:S(2)}) copy-start(s32[64,1]{0,1:T(1,128)} %param.9) | copy-start | bytes 772

commit v6 on v5

--- a/solution.py
+++ b/solution.py
@@ -427,7 +427,7 @@
         functools.partial(kernel, n, pairs),
         out_shape=jax.ShapeDtypeStruct((n, 9, 16, 256), BF16),
         in_specs=[pl.BlockSpec(memory_space=pltpu.HBM)] * 6,
-        out_specs=pl.BlockSpec(memory_space=pltpu.VMEM),
+        out_specs=pl.BlockSpec(memory_space=pl.ANY),
         scratch_shapes=[
             pltpu.VMEM((rows, SAMPLES), BF16),
             pltpu.VMEM((1, pairs), jnp.int32),
@@ -454,7 +454,7 @@
             pltpu.SemaphoreType.DMA((2,)),
         ],
         compiler_params=pltpu.CompilerParams(
-            collective_id=0, has_side_effects=True, vmem_limit_bytes=44 * 2**20
+            collective_id=0, has_side_effects=True, vmem_limit_bytes=56 * 2**20
         ),
     )(
         windows[0].transpose(1, 0, 2).reshape(rows, SAMPLES),

time: 59 us -> 55.9 us (0.947)
  local copies, waits for them, and re-layouts: 6.27 us -> 0 us
  Pallas kernels: 50.8 us -> 52.8 us
  other arithmetic: 1.74 us -> 3.01 us
    unnamed x10 -> x0, local copies, waits for them, and re-layouts: 6.27 us -> none
    pallas_call x1, Pallas kernels: 50.8 us -> 52.8 us  [shards(): pl.pallas_call(functools.partial(kernel, n, pairs), out_shape=jax.ShapeDt...]
    div x1, other arithmetic: 1.74 us -> 3.01 us  [shards(): return received.astype(F32) / jnp.sqrt(F32(2 * NB))]
where the time goes in v6:
time: 55.9 us; the launch traced here: 55.8 us
  Pallas kernels  52.8 us (94%)
  other arithmetic  3.01 us (5%)
    pallas_call x1, Pallas kernels, shards(): pl.pallas_call(functools.partial(kernel, n, pairs), out_shape=jax.ShapeDt...  52.8 us
    div x1, other arithmetic, shards(): return received.astype(F32) / jnp.sqrt(F32(2 * NB))  3.01 us

profile of v6, /device:TPU:0, one launch (start us, length us, event | category | flops | bytes accessed | tf_op | source)
XLA Modules:
  0.0 55.8 jit_solution(1366021421469197423)
XLA Ops:
  0.0 52.8 %shard_map.64 = bf16[16,9,16,256]{3,2,1,0:T(8,128)(2,1)} custom-call(bf16[24,4096]{1,0:T(8,128)(2,1)} %bitcast.13, s32[1,64]{1,0:T(1,128)} %bitcast.14, s32[1,64]{1,0:T(1,128)} %bitcast.15, s32[1,64]{1,0:T(1,128)} %bitcast.16, bf16[8,2048,256]{2,1,0:T(8,128)(2,1)} %constant.7.clone.fwd_hbm, bf16[4,4096,256]{2,1,0:T(8,128)(2,1)} %constant.8.clone.inv_hbm), custom_call_target="tpu_custom_call" | custom-call | tf_op jit(solution)/shard_map/pallas_call | solution.py:426
  52.8 3.0 %convert_multiply_fusion = f32[16,9,16,256]{3,2,1,0:T(8,128)} fusion(bf16[16,9,16,256]{3,2,1,0:T(8,128)(2,1)} %shard_map.64), kind=kLoop, calls=%fused_computation | loop fusion | flops 1179648 | bytes 3538944 | tf_op jit(solution)/shard_map/div | solution.py:468

commit v7 on v6

--- a/solution.py
+++ b/solution.py
@@ -129,9 +129,9 @@
 
 
 def kernel(
-    n, pairs, x_hbm, first_hbm, second_hbm, owner_hbm, fwd_hbm, inv_hbm, out_ref,
-    x_ref, first_ref, second_ref, owner_ref, in_sem, fwd_v, inv_v, xm, spec, white, a_v, b_v, early, cross, lagged, outgoing,
-    fwd_sem, inv_sem, near_send, near_recv, far_send, far_recv, own_sem,
+    n, pairs, x_hbm, first_hbm, second_hbm, owner_hbm, fwd_hbm, inv_hbm, out_hbm,
+    x_ref, first_ref, second_ref, owner_ref, in_sem, fwd_v, inv_v, xm, spec, white, a_v, b_v, early, cross, lagged, outgoing, landed, stacked,
+    fwd_sem, inv_sem, near_send, near_recv, far_send, far_recv, own_sem, out_sem,
 ):
     me = lax.axis_index("sens")
     hour = lax.axis_index("hour")
@@ -366,13 +366,13 @@
 
     def far_copy(part, source, dst):
         return pltpu.make_async_remote_copy(
-            src_ref=outgoing.at[dst, spans[part]], dst_ref=out_ref.at[source, spans[part]],
+            src_ref=outgoing.at[dst, spans[part]], dst_ref=landed.at[source, spans[part]],
             send_sem=far_send.at[part, dst], recv_sem=far_recv.at[part, source],
             device_id=(dst, hour), device_id_type=MESH,
         )
 
     def own_copy(part):
-        return pltpu.make_async_copy(outgoing.at[me, spans[part]], out_ref.at[me, spans[part]], own_sem.at[part])
+        return pltpu.make_async_copy(outgoing.at[me, spans[part]], landed.at[me, spans[part]], own_sem.at[part])
 
     for part in range(2):
         for lag_half, units, skip in ((hour, ((0, 2, 4), (6, 8))[part], 0), (other, ((1, 3), (5, 7))[part], hour)):
@@ -402,17 +402,40 @@
         lax.fori_loop(0, 8, send, 0)
         own_copy(part).start()
 
+    def out_copy(source):
+        here = pl.ds(pl.multiple_of(source * 8, 8), 8)
+        return pltpu.make_async_copy(stacked.at[here], out_hbm.at[here], out_sem.at[source])
+
+    def widen(source):
+        here = pl.ds(pl.multiple_of(source * 8, 8), 8)
+        for unit in range(9):
+            both = landed[source, unit].astype(F32) * (1.0 / (2 * NB) ** 0.5)
+            stacked[here, unit * 512:unit * 512 + 256] = both[:8]
+            stacked[here, unit * 512 + 256:(unit + 1) * 512] = both[8:]
+        out_copy(source).start()
+
+    for part in range(2):
+        own_copy(part).wait()
+    widen(me)
+
     def finish(step, carry):
         peer = lax.rem(me + step, n)
         for part in range(2):
-            copy = far_copy(part, peer, peer)
-            copy.wait_send()
-            copy.wait_recv()
+            far_copy(part, peer, peer).wait_recv()
+        widen(peer)
         return carry
 
     lax.fori_loop(1, n, finish, 0)
-    for part in range(2):
-        own_copy(part).wait()
+
+    def settle(step, carry):
+        peer = lax.rem(me + step, n)
+        for part in range(2):
+            far_copy(part, peer, peer).wait_send()
+        out_copy(peer).wait()
+        return carry
+
+    lax.fori_loop(1, n, settle, 0)
+    out_copy(me).wait()
     for p in range(PIECES):
         for copy in (copy_far(p), copy_hour(p), copy_both(p), odd_own(p), odd_other(p)):
             copy.wait_send()
@@ -423,9 +446,9 @@
     rows = windows.shape[1] * COMPS
     pairs = pair_first.shape[0]
     fwd, inv = (jnp.asarray(table) for table in folded_tables())
-    received = pl.pallas_call(
+    return pl.pallas_call(
         functools.partial(kernel, n, pairs),
-        out_shape=jax.ShapeDtypeStruct((n, 9, 16, 256), BF16),
+        out_shape=jax.ShapeDtypeStruct((8 * n, WIDTH // 2), F32),
         in_specs=[pl.BlockSpec(memory_space=pltpu.HBM)] * 6,
         out_specs=pl.BlockSpec(memory_space=pl.ANY),
         scratch_shapes=[
@@ -445,6 +468,8 @@
             pltpu.VMEM((5 * pairs, 2 * NB), BF16),
             pltpu.VMEM((2, 3 * pairs, 256), BF16),
             pltpu.VMEM((n, 9, 16, 256), BF16),
+            pltpu.VMEM((n, 9, 16, 256), BF16),
+            pltpu.VMEM((8 * n, WIDTH // 2), F32),
             pltpu.SemaphoreType.DMA((CHUNKS,)),
             pltpu.SemaphoreType.DMA((4,)),
             pltpu.SemaphoreType.DMA((5, PIECES)),
@@ -452,6 +477,7 @@
             pltpu.SemaphoreType.DMA((2, n)),
             pltpu.SemaphoreType.DMA((2, n)),
             pltpu.SemaphoreType.DMA((2,)),
+            pltpu.SemaphoreType.DMA((n,)),
         ],
         compiler_params=pltpu.CompilerParams(
             collective_id=0, has_side_effects=True, vmem_limit_bytes=56 * 2**20
@@ -464,8 +490,6 @@
         fwd,
         inv,
     )
-    received = received.reshape(n, 9, 2, 8, 256).transpose(0, 3, 1, 2, 4).reshape(n * 8, WIDTH // 2)
-    return received.astype(F32) / jnp.sqrt(F32(2 * NB))
 
 
 def solution(mesh):

time: 55.9 us -> 57.1 us (1.021)
  local copies, waits for them, and re-layouts: 0 us -> 3.24 us
  other arithmetic: 3.01 us -> 0 us
  Pallas kernels: 52.8 us -> 53.7 us
    unnamed x0 -> x1, local copies, waits for them, and re-layouts: none -> 3.24 us
    div x1 -> x0, other arithmetic: 3.01 us -> none  [shards(): return received.astype(F32) / jnp.sqrt(F32(2 * NB))]
    pallas_call x1, Pallas kernels: 52.8 us -> 53.7 us  [shards(): pl.pallas_call(functools.partial(kernel, n, pairs), out_shape=jax.ShapeDt...]
where the time goes in v7:
time: 57.1 us; the launch traced here: 56.9 us
  Pallas kernels  53.7 us (94%)
  local copies, waits for them, and re-layouts  3.24 us (6%)
    pallas_call x1, Pallas kernels, shards(): pl.pallas_call(functools.partial(kernel, n, pairs), out_shape=jax.ShapeDt...  53.7 us
    unnamed x1, local copies, waits for them, and re-layouts  3.24 us

profile of v7, /device:TPU:0, one launch (start us, length us, event | category | flops | bytes accessed | tf_op | source)
XLA Modules:
  0.0 56.9 jit_solution(12964047828503499107)
XLA Ops:
  0.0 53.7 %shard_map.64 = f32[128,4608]{1,0:T(8,128)} custom-call(bf16[24,4096]{1,0:T(8,128)(2,1)} %bitcast.8, s32[1,64]{1,0:T(1,128)} %bitcast.9, s32[1,64]{1,0:T(1,128)} %bitcast.10, s32[1,64]{1,0:T(1,128)} %bitcast.11, bf16[8,2048,256]{2,1,0:T(8,128)(2,1)} %constant.4.clone.fwd_hbm, bf16[4,4096,256]{2,1,0:T(8,128)(2,1)} %constant.5.clone.inv_hbm), custom_call_target="tpu_custom_call" | custom-call | tf_op jit(solution)/shard_map/pallas_call | solution.py:449
  53.7 3.2 %copy.8 = f32[128,4608]{1,0:T(8,128)} copy(f32[128,4608]{1,0:T(8,128)} %shard_map.64) | data formatting | bytes 4718592

commit v8 on v6

--- a/solution.py
+++ b/solution.py
@@ -427,7 +427,7 @@
         functools.partial(kernel, n, pairs),
         out_shape=jax.ShapeDtypeStruct((n, 9, 16, 256), BF16),
         in_specs=[pl.BlockSpec(memory_space=pltpu.HBM)] * 6,
-        out_specs=pl.BlockSpec(memory_space=pl.ANY),
+        out_specs=pl.BlockSpec(memory_space=pltpu.VMEM),
         scratch_shapes=[
             pltpu.VMEM((rows, SAMPLES), BF16),
             pltpu.VMEM((1, pairs), jnp.int32),

time: 55.9 us -> 56.8 us (1.016)
  Pallas kernels: 52.8 us -> 53.7 us
    pallas_call x1, Pallas kernels: 52.8 us -> 53.7 us  [shards(): pl.pallas_call(functools.partial(kernel, n, pairs), out_shape=jax.ShapeDt...]
where the time goes in v8:
time: 56.8 us; the launch traced here: 56.7 us
  Pallas kernels  53.7 us (95%)
  other arithmetic  3.01 us (5%)
    pallas_call x1, Pallas kernels, shards(): pl.pallas_call(functools.partial(kernel, n, pairs), out_shape=jax.ShapeDt...  53.7 us
    div x1, other arithmetic, shards(): return received.astype(F32) / jnp.sqrt(F32(2 * NB))  3.01 us

profile of v8, /device:TPU:0, one launch (start us, length us, event | category | flops | bytes accessed | tf_op | source)
XLA Modules:
  0.0 56.7 jit_solution(1949101140141685419)
XLA Ops:
  0.0 53.7 %shard_map.64 = bf16[16,9,16,256]{3,2,1,0:T(8,128)(2,1)} custom-call(bf16[24,4096]{1,0:T(8,128)(2,1)} %bitcast.13, s32[1,64]{1,0:T(1,128)} %bitcast.14, s32[1,64]{1,0:T(1,128)} %bitcast.15, s32[1,64]{1,0:T(1,128)} %bitcast.16, bf16[8,2048,256]{2,1,0:T(8,128)(2,1)} %constant.7.clone.fwd_hbm, bf16[4,4096,256]{2,1,0:T(8,128)(2,1)} %constant.8.clone.inv_hbm), custom_call_target="tpu_custom_call" | custom-call | tf_op jit(solution)/shard_map/pallas_call | solution.py:426
  53.7 3.0 %convert_multiply_fusion = f32[16,9,16,256]{3,2,1,0:T(8,128)} fusion(bf16[16,9,16,256]{3,2,1,0:T(8,128)(2,1)} %shard_map.64), kind=kLoop, calls=%fused_computation | loop fusion | flops 1179648 | bytes 3538944 | tf_op jit(solution)/shard_map/div | solution.py:468
